TPU v7x, 128 devices: a whole 4x4x4 slice. The times are simulated.
128 devices in a mesh: replica: 8 (over z, y_hi), fsdp: 2 (over y_lo), context: 8 (over x, core).
Axes of the slice: x: 4, y: 4 (y_hi: 2, y_lo: 2; y = y_hi * 2 + y_lo), z: 4, core: 2. Of those that a mesh axis runs over, the one named last changes fastest.
Arguments:
- queries: bfloat16 [8, 4096, 5120], P('replica', ('fsdp', 'context')), may hold values from -7 to 7
- keys: bfloat16 [8, 4096, 1024], P('replica', ('fsdp', 'context')), may hold values from -7 to 7
- values: bfloat16 [8, 4096, 1024], P('replica', ('fsdp', 'context')), may hold values from -6 to 6
- valid_length: int32 [8], P('replica'), may hold values from 2048 to 4096
- norm_gain: float32 [5120], replicated, may hold values from 0.1 to 1.9
- value_head: float32 [5120], replicated, may hold values from -0.078125 to 0.078125
- policy_in: bfloat16 [8, 4096, 1536], P('replica', ('fsdp', 'context')), may hold values from -6 to 6
- cotangent: bfloat16 [8, 4096, 2048], P('replica', ('fsdp', 'context')), may hold values from -6 to 6
- qkv_weight: bfloat16 [1536, 2048], P('fsdp'), may hold values from -0.125 to 0.125
Outputs:
- attn_out: bfloat16 [8, 4096, 5120], P('replica', ('fsdp', 'context'))
- advantage: float32 [8], P('replica')
- input_grad: bfloat16 [8, 4096, 1536], P('replica', ('fsdp', 'context'))
- weight_grad: float32 [1536, 2048], P('fsdp')
All inputs are finite; a program needn't handle non-finite values.
Results may differ from a plain program's by a relative error of at most 0.018.
Values may be sent and summed in bfloat16 or wider, within the bound.
No kernel may reach another device: no remote copies, remote signals or barrier semaphores. Data moves between devices by JAX's collectives and lax.ppermute only.
A program may use at most 192 MiB of HBM per device.

v0:
```python
import math

import jax
import jax.numpy as jnp
from jax import lax
from jax.experimental import pallas as pl
from jax.experimental.pallas import tpu as pltpu
from jax.sharding import PartitionSpec as P

HEAD_DIM = 128
GROUP = 5
BLOCK = 512
HALF = BLOCK // 2
NEG = -1e30
FAR = 1 << 24
LOG2_SCALE = math.log2(math.e) / math.sqrt(HEAD_DIM)
BF = jnp.bfloat16
F32 = jnp.float32


VMEM_BYTES = 36 * 1024 * 1024
ANY = pl.BlockSpec(memory_space=pl.ANY)
PARAMS = pltpu.CompilerParams(vmem_limit_bytes=VMEM_BYTES)
TINY = pl.CostEstimate(flops=1, bytes_accessed=1, transcendentals=0)


def split_kv(info, keys, values):
    rows, half = keys.shape[0], keys.shape[1] // 2

    def kernel(info_ref, k_send, k_keep, v_send, v_keep, send_ref, keep_ref):
        send_ref[0], send_ref[1] = k_send[...], v_send[...]
        keep_ref[0], keep_ref[1] = k_keep[...], v_keep[...]

    there = pl.BlockSpec((rows, half), lambda i, info: (0, 1 - info[2]))
    here = pl.BlockSpec((rows, half), lambda i, info: (0, info[2]))
    whole = pl.BlockSpec((2, rows, half), lambda i, info: (0, 0, 0))
    shape = jax.ShapeDtypeStruct((2, rows, half), BF)
    return pl.pallas_call(
        kernel,
        grid_spec=pltpu.PrefetchScalarGridSpec(
            num_scalar_prefetch=1,
            grid=(1,),
            in_specs=[there, here, there, here],
            out_specs=(whole, whole),
        ),
        out_shape=(shape, shape),
        compiler_params=PARAMS,
        cost_estimate=TINY,
        name="split_kv",
    )(info, keys, keys, values, values)


def policy_terms(info, inputs, cotangent, after):
    rows, wide = inputs.shape
    half, step = cotangent.shape[1] // 2, 256

    def kernel(info_ref, in_ref, there_ref, here_ref, *refs):
        send_ref, keep_ref = refs[-2:]
        pos = info_ref[0] + lax.broadcasted_iota(jnp.int32, (rows, half), 0)
        for ref, out in ((there_ref, send_ref), (here_ref, keep_ref)):
            masked = jnp.where(pos < info_ref[1], ref[...], jnp.zeros((rows, half), BF))
            out[...] = lax.dot_general(
                in_ref[...], masked, (((0,), (0,)), ((), ())), preferred_element_type=F32
            ).astype(BF)

    out = pl.BlockSpec((step, half), lambda i, info: (i, 0))
    shape = jax.ShapeDtypeStruct((wide, half), BF)
    return pl.pallas_call(
        kernel,
        grid_spec=pltpu.PrefetchScalarGridSpec(
            num_scalar_prefetch=1,
            grid=(wide // step,),
            in_specs=[
                pl.BlockSpec((rows, step), lambda i, info: (0, i)),
                pl.BlockSpec((rows, half), lambda i, info: (0, 1 - info[2])),
                pl.BlockSpec((rows, half), lambda i, info: (0, info[2])),
            ]
            + [ANY] * len(after),
            out_specs=(out, out),
        ),
        out_shape=(shape, shape),
        compiler_params=PARAMS,
        cost_estimate=TINY,
        name="policy_terms",
    )(info, inputs, cotangent, cotangent, *after)


def combine(weights, terms, after):
    n, (rows, cols) = len(terms), terms[0].shape

    def kernel(w_ref, *refs):
        total = refs[0][...].astype(F32) * w_ref[0]
        for i in range(1, n):
            total += refs[i][...].astype(F32) * w_ref[i]
        refs[-1][...] = total.astype(BF)

    step = rows // 4
    spec = pl.BlockSpec((step, cols), lambda i, w: (i, 0))
    return pl.pallas_call(
        kernel,
        grid_spec=pltpu.PrefetchScalarGridSpec(
            num_scalar_prefetch=1,
            grid=(rows // step,),
            in_specs=[spec] * n + [ANY] * len(after),
            out_specs=spec,
        ),
        out_shape=jax.ShapeDtypeStruct((rows, cols), BF),
        compiler_params=PARAMS,
        cost_estimate=TINY,
        name="combine",
    )(weights, *terms, *after)


def place(info, pieces):
    n, (rows, cols) = len(pieces), pieces[0].shape
    chips = n // 2

    def kernel(info_ref, *refs):
        for i in range(n):

            @pl.when(pl.program_id(0) == i)
            def _():
                refs[n][...] = refs[i][...].astype(F32)

    return pl.pallas_call(
        kernel,
        grid_spec=pltpu.PrefetchScalarGridSpec(
            num_scalar_prefetch=1,
            grid=(n,),
            in_specs=[pl.BlockSpec((rows, cols), lambda i, info: (0, 0))] * n,
            out_specs=pl.BlockSpec(
                (rows, cols), lambda i, info: (info[i // 2], lax.rem(info[chips] + i, 2))
            ),
        ),
        out_shape=jax.ShapeDtypeStruct((chips * rows, 2 * cols), F32),
        compiler_params=PARAMS,
        cost_estimate=TINY,
        name="place",
    )(info, *pieces)


def add(info, sums, rows, steps, after):
    cols = sums[0][0][0].shape[1]
    counts = [len(terms) for terms in sums]
    n = sum(counts)

    def kernel(info_ref, *refs):
        start = 0
        for out, count in zip(refs[len(refs) - len(sums) :], counts):
            total = refs[start][...].astype(F32)
            for ref in refs[start + 1 : start + count]:
                total += ref[...].astype(F32)
            start += count
            out[...] = total.astype(BF)

    def spec(at):
        return pl.BlockSpec((rows, cols), lambda i, info: (at(i, info), 0))

    flat = [term for terms in sums for term in terms]
    shape = jax.ShapeDtypeStruct((rows * steps, cols), BF)
    return pl.pallas_call(
        kernel,
        grid_spec=pltpu.PrefetchScalarGridSpec(
            num_scalar_prefetch=1,
            grid=(steps,),
            in_specs=[spec(at) for _, at in flat] + [ANY] * len(after),
            out_specs=[spec(lambda i, info: i)] * len(sums),
        ),
        out_shape=[shape] * len(sums),
        compiler_params=PARAMS,
        cost_estimate=TINY,
        name="add",
    )(info, *(array for array, _ in flat), *after)


def pick(info, array, block, at, after):
    def kernel(info_ref, in_ref, *refs):
        refs[-1][...] = in_ref[...]

    zero = (0,) * len(block)
    return pl.pallas_call(
        kernel,
        grid_spec=pltpu.PrefetchScalarGridSpec(
            num_scalar_prefetch=1,
            grid=(1,),
            in_specs=[pl.BlockSpec(block, lambda i, info: at(info))] + [ANY] * len(after),
            out_specs=pl.BlockSpec(block, lambda i, info: zero),
        ),
        out_shape=jax.ShapeDtypeStruct(block, array.dtype),
        compiler_params=PARAMS,
        cost_estimate=TINY,
        name="pick",
    )(info, array, *after)


def in_hbm(array):
    return pltpu.with_memory_space_constraint(array, pltpu.HBM)


def attend(info, q, heads, pieces, joined, state, last, flops, after=()):
    n, n_after, first = len(pieces), len(after), not state
    wide = GROUP * HEAD_DIM

    def kernel(info_ref, here_ref, got_ref, *refs):
        kv_refs, refs = refs[: 2 * n], refs[2 * n :]
        if not first:
            acc_in, ml_in = refs[:2]
            refs = refs[2:]
        refs = refs[n_after:]
        out_a, out_b, q_s, k_s, v_s, acc_s, m_s = refs
        q_base, length, core = info_ref[0], info_ref[1], info_ref[2]
        for h in range(GROUP):
            cols = slice(h * HEAD_DIM, (h + 1) * HEAD_DIM)
            for part, ref in enumerate((here_ref, got_ref)):
                at = slice(part * HALF, (part + 1) * HALF)
                scaled = ref[:, cols].astype(F32) * LOG2_SCALE
                high = scaled.astype(BF)
                q_s[h, at, :HEAD_DIM] = high
                q_s[h, at, HEAD_DIM:] = (scaled - high.astype(F32)).astype(BF)
            if first:
                acc_s[h] = jnp.zeros((BLOCK, 2 * HEAD_DIM), F32)
                m_s[h] = jnp.full((BLOCK, HEAD_DIM), NEG, F32)
            else:
                acc_s[h, :, :HEAD_DIM] = acc_in[0, :, cols]
                m_s[h] = jnp.broadcast_to(ml_in[0, :, h : h + 1], (BLOCK, HEAD_DIM))
                acc_s[h, :, HEAD_DIM:] = jnp.broadcast_to(
                    ml_in[0, :, 8 + h : 9 + h], (BLOCK, HEAD_DIM)
                )
        for i in range(n):
            at = slice(i * BLOCK, (i + 1) * BLOCK)
            k_s[at, :HEAD_DIM] = kv_refs[2 * i][0]
            k_s[at, HEAD_DIM:] = kv_refs[2 * i][0]
            v_s[at, :HEAD_DIM] = kv_refs[2 * i + 1][0]
            v_s[at, HEAD_DIM:] = jnp.ones((BLOCK, HEAD_DIM), BF)

        def tiles(i, count, keep):
            keys = count * BLOCK
            at = pl.ds(pl.multiple_of(i * BLOCK, BLOCK), keys)
            kk, v1 = k_s[at, :], v_s[at, :]

            def scores(h):
                s = lax.dot_general(
                    q_s[h], kk, (((1,), (1,)), ((), ())), preferred_element_type=F32
                )
                return s if keep is None else jnp.where(keep, s, NEG)

            s = scores(0)
            for h in range(GROUP):
                later = scores(h + 1) if h + 1 < GROUP else None
                m_old = m_s[h]
                m_new = jnp.maximum(m_old, jnp.max(s, axis=1, keepdims=True))
                p = jnp.exp2(s - jnp.tile(m_new, (1, keys // HEAD_DIM)))
                pv = jnp.dot(p.astype(BF), v1, preferred_element_type=F32)
                m_s[h] = m_new
                acc_s[h] = acc_s[h] * jnp.tile(jnp.exp2(m_old - m_new), (1, 2)) + pv
                s = later

        taken = []
        for begin, count in joined:
            far = info_ref[3 + begin]
            for i in range(begin + 1, begin + count):
                far = jnp.maximum(far, info_ref[3 + i])
            together = (far < q_base) & (far + BLOCK <= length)
            taken.append((begin, count, together))

            @pl.when(together)
            def _():
                tiles(begin, count, None)

        @pl.loop(0, n)
        def _(i):
            base = info_ref[3 + i]
            use = (base <= q_base) & (base < length)
            for begin, count, together in taken:
                use &= jnp.logical_not(together & (i >= begin) & (i < begin + count))

            @pl.when(use)
            def _():
                row = lax.broadcasted_iota(jnp.int32, (BLOCK, BLOCK), 0)
                col = lax.broadcasted_iota(jnp.int32, (BLOCK, BLOCK), 1)
                row = q_base + ((row + HALF * core) & (BLOCK - 1))
                col = base + ((col + HALF * core) & (BLOCK - 1))
                tiles(i, 1, (col <= row) & (col < length))

        if last:
            for h in range(GROUP):
                cols = slice(h * HEAD_DIM, (h + 1) * HEAD_DIM)
                mixed = (acc_s[h, :, :HEAD_DIM] / acc_s[h, :, HEAD_DIM:]).astype(BF)
                out_a[:, cols] = mixed[:HALF]
                out_b[:, cols] = mixed[HALF:]
        else:
            lane = lax.broadcasted_iota(jnp.int32, (BLOCK, HEAD_DIM), 1)
            ml = jnp.zeros((BLOCK, HEAD_DIM), F32)
            for h in range(GROUP):
                out_a[0, :, h * HEAD_DIM : (h + 1) * HEAD_DIM] = acc_s[h, :, :HEAD_DIM]
                ml = jnp.where(lane == h, m_s[h], ml)
                ml = jnp.where(lane == 8 + h, acc_s[h, :, HEAD_DIM:], ml)
            out_b[0] = ml

    def kv_spec(index):
        return pl.BlockSpec((1, BLOCK, HEAD_DIM), lambda g, info: (index, 0, g))

    operands, kv_specs = [], []
    for kv in pieces:
        operands += [in_hbm(kv)] * 2
        kv_specs += [kv_spec(0), kv_spec(1)]
    q_specs = [
        pl.BlockSpec((HALF, wide), lambda g, info: (0, info[2] * heads + g)),
        pl.BlockSpec((HALF, wide), lambda g, info: (0, g)),
    ]
    out_spec = pl.BlockSpec((HALF, wide), lambda g, info: (0, g))
    acc_spec = pl.BlockSpec((1, BLOCK, wide), lambda g, info: (g, 0, 0))
    ml_spec = pl.BlockSpec((1, BLOCK, HEAD_DIM), lambda g, info: (g, 0, 0))
    acc_shape = pltpu.HBM((heads, BLOCK, wide), F32)
    ml_shape = pltpu.HBM((heads, BLOCK, HEAD_DIM), F32)
    out_shape = jax.ShapeDtypeStruct((HALF, heads * wide), BF)
    return pl.pallas_call(
        kernel,
        grid_spec=pltpu.PrefetchScalarGridSpec(
            num_scalar_prefetch=1,
            grid=(heads,),
            in_specs=q_specs
            + kv_specs
            + ([] if first else [acc_spec, ml_spec])
            + [ANY] * n_after,
            out_specs=(out_spec, out_spec) if last else (acc_spec, ml_spec),
            scratch_shapes=[
                pltpu.VMEM((GROUP, BLOCK, 2 * HEAD_DIM), BF),
                pltpu.VMEM((n * BLOCK, 2 * HEAD_DIM), BF),
                pltpu.VMEM((n * BLOCK, 2 * HEAD_DIM), BF),
                pltpu.VMEM((GROUP, BLOCK, 2 * HEAD_DIM), F32),
                pltpu.VMEM((GROUP, BLOCK, HEAD_DIM), F32),
            ],
        ),
        out_shape=(out_shape, out_shape) if last else (acc_shape, ml_shape),
        compiler_params=PARAMS,
        cost_estimate=pl.CostEstimate(
            flops=flops, bytes_accessed=1, transcendentals=0
        ),
        name="attend",
    )(info, *(in_hbm(a) for a in q), *operands, *(in_hbm(a) for a in state), *after)


def finish(info, own, other, gain, head, after):
    rows, half = own.shape

    def kernel(info_ref, own_ref, other_ref, gain_ref, head_ref, *refs):
        out_ref, sum_ref = refs[-2:]
        base, length, core = info_ref[0], info_ref[1], info_ref[2]
        squares = jnp.zeros((rows, 1), F32)
        score = jnp.zeros((rows, 1), F32)
        for ref, side in ((own_ref, core), (other_ref, 1 - core)):
            cols = pl.ds(pl.multiple_of(side * half, half), half)
            part = ref[...]
            out_ref[:, cols] = part
            part = part.astype(F32)
            squares += jnp.sum(part * part, axis=1, keepdims=True)
            score += jnp.sum(part * (gain_ref[:, cols] * head_ref[:, cols]), axis=1, keepdims=True)
        score = score * lax.rsqrt(squares / (2 * half) + 1e-6)
        pos = base + lax.broadcasted_iota(jnp.int32, (rows, 1), 0)
        score = jnp.where(pos < length, score, 0.0)
        sum_ref[...] = jnp.broadcast_to(jnp.sum(score, axis=0, keepdims=True), (8, HEAD_DIM))

    return pl.pallas_call(
        kernel,
        grid_spec=pltpu.PrefetchScalarGridSpec(
            num_scalar_prefetch=1,
            grid=(1,),
            in_specs=[
                pl.BlockSpec((rows, half), lambda g, _: (0, 0)),
                pl.BlockSpec((rows, half), lambda g, _: (0, 0)),
                pl.BlockSpec((1, 2 * half), lambda g, _: (0, 0)),
                pl.BlockSpec((1, 2 * half), lambda g, _: (0, 0)),
            ]
            + [ANY] * len(after),
            out_specs=(
                pl.BlockSpec((rows, 2 * half), lambda g, _: (0, 0)),
                pl.BlockSpec((8, HEAD_DIM), lambda g, _: (0, 0)),
            ),
        ),
        out_shape=(
            jax.ShapeDtypeStruct((rows, 2 * half), BF),
            jax.ShapeDtypeStruct((8, HEAD_DIM), F32),
        ),
        compiler_params=PARAMS,
        cost_estimate=TINY,
        name="finish",
    )(info, own, other, gain[None], head[None], *after)


def shards(
    queries, keys, values, valid_length, norm_gain, value_head, policy_in, cotangent, qkv_weight
):
    n_rep, n_fsdp, n_ctx = (lax.axis_size(a) for a in ("replica", "fsdp", "context"))
    n_x, n_z = n_ctx // 2, n_rep // 2
    f, ctx, rep = lax.axis_index("fsdp"), lax.axis_index("context"), lax.axis_index("replica")
    x, core = ctx // 2, ctx % 2
    length = valid_length[0]
    rows = queries.shape[1]

    swap = [(i, i ^ 1) for i in range(n_ctx)]

    def along_x(step, planes):
        return [
            (p * n_ctx + i, p * n_ctx + (i + 2 * step) % n_ctx)
            for p in planes
            for i in range(n_ctx)
        ]

    def move(array, step, planes):
        return lax.ppermute(array, ("fsdp", "context"), along_x(step, planes))

    def side(array, which, axis):
        size = array.shape[axis] // 2
        return lax.dynamic_slice_in_dim(array, which * size, size, axis)

    tok_base = (f * n_ctx + ctx) * rows
    tok_info = jnp.stack([tok_base, length, core, f, x]).astype(jnp.int32)

    tok_base = (f * n_ctx + ctx) * rows
    tok_info = jnp.stack([tok_base, length, core, f, x]).astype(jnp.int32)
    kv_heads = keys.shape[2] // HEAD_DIM // 2

    kv_send, kv_keep = split_kv(tok_info, keys[0], values[0])
    kv_own = jnp.concatenate([kv_keep, lax.ppermute(kv_send, "context", swap)], axis=1)
    p_send, p_keep = policy_terms(tok_info, policy_in[0], cotangent[0], (kv_keep,))
    q_here = queries[0]
    q_send = pick(
        tok_info, q_here, (rows, q_here.shape[1] // 2), lambda info: (0, 1 - info[2]), (p_send,)
    )
    q_got = lax.ppermute(q_send, "context", swap)

    both, later = range(n_fsdp), [1]
    cross = {0: lax.ppermute(kv_own, "fsdp", [(0, 1)])}
    ring = {d: move(kv_own, d, both) for d in (1, 3, 2)}
    for d in (1, 3, 2):
        cross[d] = move(cross[0], d, later)

    pairs = []
    for r in range(n_rep):
        for g in range(n_fsdp):
            y_to = ((r % 2) * 2 + g) ^ 3
            pairs.append((r * 2 + g, ((r // 2) * 2 + y_to // 2) * 2 + y_to % 2))
    weight_other = lax.ppermute(qkv_weight, ("replica", "fsdp"), pairs)

    def pos(plane, d):
        return (plane * n_x + (x - d) % n_x) * BLOCK

    def near(*distances):
        return [pos(f, d) for d in distances]

    def other(*distances):
        return [jnp.where(f == 1, pos(0, d), FAR) for d in distances]

    def step(positions, pieces, joined, state, flops, after):
        items = [pos(f, 0), length, core] + positions
        info = jnp.stack([jnp.asarray(i, jnp.int32) for i in items])
        return attend(info, (q_here, q_got), kv_heads, pieces, joined, state, bool(state), flops, after)

    chunk = p_keep.shape[0] // (n_fsdp * n_x)
    got = lax.ppermute(p_send, "context", swap)
    p_send, p_keep = add(
        tok_info,
        [
            [(a, lambda i, info: (1 - info[3]) * n_x + i) for a in (p_keep, got)],
            [(a, lambda i, info: info[3] * n_x + i) for a in (p_keep, got)],
        ],
        chunk,
        n_x,
        (cross[0],),
    )
    got = lax.ppermute(p_send, "fsdp", [(0, 1), (1, 0)])

    state = step(
        other(0) + near(1, 3, 2, 0),
        [cross[0], ring[1], ring[3], ring[2], kv_own],
        [(0, 2), (2, 2)],
        (),
        flops=24 * 10**9,
        after=(p_send,),
    )
    chunks = add(
        tok_info,
        [
            [(a, lambda i, info, d=d: lax.rem(info[4] + d, n_x)) for a in (p_keep, got)]
            for d in range(n_x)
        ],
        chunk,
        1,
        state[1:],
    )
    parts = [chunks[0]] + [move(chunks[d], d, both) for d in range(1, n_x)]
    mixed = step(
        other(1, 3, 2),
        [cross[1], cross[3], cross[2]],
        [(0, 3)],
        state,
        flops=24 * 10**9,
        after=(chunks[0],),
    )
    (total,) = add(tok_info, [[(a, lambda i, info: 0) for a in parts]], chunk, 1, mixed[:1])
    mixed_there = pick(tok_info, mixed[1], mixed[1].shape, lambda info: (0, 0), (total,))

    z, y_hi = rep // 2, rep % 2

    def along_z(array, dz):
        pairs = [(r, (r + 2 * dz) % n_rep) for r in range(n_rep)]
        return lax.ppermute(array, "replica", pairs) if dz else array

    terms = [along_z(total, dz) for dz in range(n_z)]
    sources = jnp.stack([((z - dz) % n_z) * 2 + y_hi for dz in range(n_z)])
    attn_out, reward_sum = finish(
        tok_info,
        mixed[0],
        lax.ppermute(mixed_there, "context", swap),
        norm_gain,
        value_head,
        (weight_other,),
    )

    valid = tok_base + jnp.arange(rows, dtype=jnp.int32) < length
    masked = jnp.where(valid[:, None], cotangent[0], jnp.zeros_like(cotangent[0]))

    def raw(weight):
        return lax.dot_general(
            masked, weight, (((1,), (1,)), ((), ())), preferred_element_type=F32
        )

    raw_own, raw_other = raw(qkv_weight), raw(weight_other)

    partial = reward_sum[:1] / jnp.sqrt(length.astype(F32))
    n_dev = n_rep * n_fsdp * n_ctx
    sums = lax.all_to_all(
        jnp.broadcast_to(partial, (n_dev, HEAD_DIM)),
        ("replica", "fsdp", "context"),
        0,
        0,
        tiled=True,
    )
    reward = jnp.sum(sums[:, 0].reshape(n_rep, n_fsdp * n_ctx), axis=1)
    mean = jnp.mean(reward)
    var = jnp.mean(reward * reward) - mean * mean
    advantages = (reward - mean) / jnp.sqrt(var + 0.25)
    advantage = lax.dynamic_slice_in_dim(advantages, rep, 1)

    weight_rows = combine(advantages[sources], terms, (raw_own, raw_other))
    beside = lax.ppermute(weight_rows, "replica", [(r, r ^ 1) for r in range(n_rep)])
    (weight_rows,) = add(
        tok_info, [[(a, lambda i, info: 0) for a in (weight_rows, beside)]], chunk, 1, ()
    )
    parts = []
    for d in (0, 1, 3, 2):
        part = move(weight_rows, d, both) if d else weight_rows
        parts += [part, lax.ppermute(part, "context", swap)]
    chips = [(x - d) % n_x for d in (0, 1, 3, 2)]
    weight_grad = place(jnp.stack(chips + [core]).astype(jnp.int32), parts)
    input_grad = jnp.where(
        f == 0,
        jnp.concatenate([raw_own, raw_other], axis=1),
        jnp.concatenate([raw_other, raw_own], axis=1),
    )
    input_grad = (advantage * input_grad).astype(BF)
    return (attn_out[None], advantage, input_grad[None], weight_grad)


def solution(mesh):
    tokens = P("replica", ("fsdp", "context"), None)
    in_specs = (tokens, tokens, tokens, P("replica"), P(), P(), tokens, tokens, P("fsdp", None))
    out_specs = (tokens, P("replica"), tokens, P("fsdp", None))
    return jax.shard_map(shards, mesh=mesh, in_specs=in_specs, out_specs=out_specs, check_vma=False)
```

profile of v0, /device:TPU:1, one launch (start us, length us, event | category | flops | bytes accessed | tf_op | source)
XLA Modules:
  0.0 240.4 jit_solution(3118236109879006292)
XLA Ops:
  1.4 1.1 copy-done.3
  2.5 1.0 copy-done.4
  3.6 0.6 split_kv.1
  4.2 0.5 copy-done.6
  4.7 4.5 %policy_terms.1 = (bf16[1536,1024]{1,0:T(8,128)(2,1)}, bf16[1536,1024]{1,0:T(8,128)(2,1)S(1)}) custom-call(s32[5]{0:T(128)S(1)} %stack.84.info_ref, bf16[256,1536]{1,0:T(8,128)(2,1)S(1)} %bitcast.60, bf16[256,2048]{1,0:T(8,128)(2,1)S(1)} %bitcast.49, bf16[256,2048]{1,0:T(8,128)(2,1)S(1)} %bitcast.50, bf16[2,256,512]{2,1,0:T(8,128)(2,1)S(1)} %get-tuple-element.20.refs_0_), custom_call_target="tpu_custom_call" | custom-call | flops 1 | bytes 1 | tf_op jit(solution)/shard_map/policy_terms/pallas_call | solution.py:68
  9.2 1.4 collective-permute-start.9
  10.7 0.9 constant_dynamic-update-slice_fusion.1
  11.5 5.0 %collective-permute-done.1 = bf16[2,256,512]{2,1,0:T(8,128)(2,1)S(1)} collective-permute-done((bf16[2,256,512]{2,1,0:T(8,128)(2,1)S(1)}, bf16[2,256,512]{2,1,0:T(8,128)(2,1)S(1)}, u32[]{:S(2)}, u32[]{:S(2)}) %collective-permute-start.1) | collective-permute-done | bytes 524320 | tf_op jit(solution)/shard_map/ppermute | solution.py:425
  16.6 0.8 constant_dynamic-update-slice_fusion.refs_8_.refs_9_
  17.4 4.3 %collective-permute-start.2 = (bf16[2,512,512]{2,1,0:T(8,128)(2,1)}, bf16[2,512,512]{2,1,0:T(8,128)(2,1)}, u32[]{:S(2)}, u32[]{:S(2)}) collective-permute-start(bf16[2,512,512]{2,1,0:T(8,128)(2,1)} %constant_dynamic-update-slice_fusion.refs_8_.refs_9_), channel_id=1, source_target_pairs={{0,8},{1,9},{2,10},{3,11},{4,12},{5,13},{6,14},{7,15},{16,24},{17,... | collective-permute-start | bytes 3145736 | tf_op jit(solution)/shard_map/ppermute | solution.py:434
  21.7 1.7 pick.2
  23.4 0.4 collective-permute-start
  23.8 1.2 collective-permute-start.6
  25.1 1.5 collective-permute-start.7
  26.5 16.9 %collective-permute-done.2.refs_4_.refs_0_.refs_1_ = bf16[2,512,512]{2,1,0:T(8,128)(2,1)} collective-permute-done((bf16[2,512,512]{2,1,0:T(8,128)(2,1)}, bf16[2,512,512]{2,1,0:T(8,128)(2,1)}, u32[]{:S(2)}, u32[]{:S(2)}) %collective-permute-start.2) | collective-permute-done | bytes 1048608 | tf_op jit(solution)/shard_map/ppermute | solution.py:434
  43.4 2.7 %collective-permute-start.8 = (bf16[2,512,512]{2,1,0:T(8,128)(2,1)}, bf16[2,512,512]{2,1,0:T(8,128)(2,1)}, u32[]{:S(2)}, u32[]{:S(2)}) collective-permute-start(bf16[2,512,512]{2,1,0:T(8,128)(2,1)} %constant_dynamic-update-slice_fusion.refs_8_.refs_9_), channel_id=1, source_target_pairs={{0,4},{1,5},{2,6},{3,7},{4,0},{5,1},{6,2},{7,3},{8,12},{9,13},{10,... | collective-permute-start | bytes 3145736 | tf_op jit(solution)/shard_map/ppermute | solution.py:411
  46.3 3.7 %collective-permute-start.15 = (bf16[768,2048]{1,0:T(8,128)(2,1)}, bf16[768,2048]{1,0:T(8,128)(2,1)}, u32[]{:S(2)}, u32[]{:S(2)}) collective-permute-start(bf16[768,2048]{1,0:T(8,128)(2,1)} %param.17), channel_id=1, source_target_pairs={{0,24},{8,16},{16,8},{24,0},{32,56},{40,48},{48,40},{56,32},{64,88... | collective-permute-start | bytes 9437192 | tf_op jit(solution)/shard_map/ppermute | solution.py:444
  50.0 3.5 %add.144 = (bf16[768,1024]{1,0:T(8,128)(2,1)S(1)}, bf16[768,1024]{1,0:T(8,128)(2,1)S(1)}) custom-call(s32[5]{0:T(128)S(1)} %stack.84.info_ref, bf16[1536,1024]{1,0:T(8,128)(2,1)S(1)} %get-tuple-element.23.refs_0_.refs_2_, bf16[1536,1024]{1,0:T(8,128)(2,1)} %collective-permute-done.9.refs_1_.refs_3_, ...), custom_call_target="tpu_custom_call" | custom-call | flops 1 | bytes 1 | tf_op jit(solution)/shard_map/add/pallas_call | solution.py:161
  53.5 0.7 collective-permute-start.3
  54.3 0.7 collective-permute-start.4
  55.0 0.7 collective-permute-start.5
  55.8 17.8 %collective-permute-done.8.refs_6_.refs_7_ = bf16[2,512,512]{2,1,0:T(8,128)(2,1)} collective-permute-done((bf16[2,512,512]{2,1,0:T(8,128)(2,1)}, bf16[2,512,512]{2,1,0:T(8,128)(2,1)}, u32[]{:S(2)}, u32[]{:S(2)}) %collective-permute-start.8) | collective-permute-done | bytes 1048608 | tf_op jit(solution)/shard_map/ppermute | solution.py:411
  73.6 16.2 %attend.2 = (f32[4,512,640]{2,1,0:T(8,128)}, f32[4,512,128]{2,1,0:T(8,128)}) custom-call(s32[8]{0:T(128)S(1)} %stack.94.info_ref, bf16[256,5120]{1,0:T(8,128)(2,1)} %bitcast.53, bf16[256,2560]{1,0:T(8,128)(2,1)} %collective-permute-done.got_ref, bf16[2,512,512]{2,1,0:T(8,128)(2,1)} %collective-permute-done.2.refs_4_.refs_0_.refs_1_, ...), custom_call_target="tpu_custom_call" | custom-call | flops 24000000000 | bytes 1 | tf_op jit(solution)/shard_map/attend/pallas_call | solution.py:317
  89.7 19.0 %collective-permute-done.10.refs_1_.refs_3_.refs_5_.refs_7_ = bf16[768,1024]{1,0:T(8,128)(2,1)S(1)} collective-permute-done((bf16[768,1024]{1,0:T(8,128)(2,1)S(1)}, bf16[768,1024]{1,0:T(8,128)(2,1)S(1)}, u32[]{:S(2)}, u32[]{:S(2)}) %collective-permute-start.10) | collective-permute-done | bytes 1572896 | tf_op jit(solution)/shard_map/ppermute | solution.py:472
  108.7 1.2 copy-done.5
  109.9 0.9 add.145
  111.1 4.5 %collective-permute-start.12 = (bf16[192,1024]{1,0:T(8,128)(2,1)S(1)}, bf16[192,1024]{1,0:T(8,128)(2,1)S(1)}, u32[]{:S(2)}, u32[]{:S(2)}) collective-permute-start(bf16[192,1024]{1,0:T(8,128)(2,1)S(1)} %get-tuple-element.32), channel_id=1, source_target_pairs={{0,4},{1,5},{2,6},{3,7},{4,0},{5,1},{6,2},{7,3},{8,12},{9,13},{10,... | collective-permute-start | bytes 1179656 | tf_op jit(solution)/shard_map/ppermute | solution.py:411
  115.6 0.9 copy-done.10
  116.5 0.3 copy-done.11
  116.9 8.9 %attend.3 = (bf16[256,2560]{1,0:T(8,128)(2,1)S(1)}, bf16[256,2560]{1,0:T(8,128)(2,1)S(1)}) custom-call(s32[6]{0:T(128)S(1)} %stack.89.info_ref, bf16[256,5120]{1,0:T(8,128)(2,1)} %bitcast.54, bf16[256,2560]{1,0:T(8,128)(2,1)} %collective-permute-done.got_ref, bf16[2,512,512]{2,1,0:T(8,128)(2,1)} %copy-done.9, bf16[2,512,512]{2,1,0:T(8,128)(2,1)} %copy-done.9, ...), custom_call_target="tpu_custom_call" | custom-call | flops 24000000000 | bytes 1 | tf_op jit(solution)/shard_map/attend/pallas_call | solution.py:317
  125.9 4.7 %collective-permute-done.12.refs_2_ = bf16[192,1024]{1,0:T(8,128)(2,1)S(1)} collective-permute-done((bf16[192,1024]{1,0:T(8,128)(2,1)S(1)}, bf16[192,1024]{1,0:T(8,128)(2,1)S(1)}, u32[]{:S(2)}, u32[]{:S(2)}) %collective-permute-start.12) | collective-permute-done | bytes 393248 | tf_op jit(solution)/shard_map/ppermute | solution.py:411
  130.6 1.5 collective-permute-done.13.refs_3_
  132.1 0.7 add.146.refs_0_
  132.8 1.7 pick.3
  134.5 2.0 collective-permute-start.14
  136.7 2.9 %fusion.3.refs_4_ = f32[256,768]{1,0:T(8,128)S(1)} fusion(bf16[768,2048]{1,0:T(8,128)(2,1)} %param.17, pred[256]{0:T(512)(128)(4,1)S(1)} %add_compare_fusion, bf16[1,256,2048]{2,1,0:T(8,128)(2,1)S(1)} %copy-done.1), kind=kOutput, calls=%fused_computation.6 | convolution fusion | flops 805830656 | bytes 4980992 | tf_op jit(solution)/shard_map/dot_general | solution.py:525
  139.7 4.2 %finish.1 = (bf16[256,5120]{1,0:T(8,128)(2,1)}, f32[8,128]{1,0:T(8,128)S(1)}) custom-call(s32[5]{0:T(128)S(1)} %stack.84.info_ref, bf16[256,2560]{1,0:T(8,128)(2,1)S(1)} %get-tuple-element.29.refs_4_.own_ref, bf16[256,2560]{1,0:T(8,128)(2,1)} %collective-permute-done.14.other_ref, f32[1,5120]{1,0:T(1,128)S(1)} %bitcast.61, f32[1,5120]{1,0:T(1,128)S(1)} %bitcast.62, ...), custom_call_target="tpu_custom_call" | custom-call | flops 1 | bytes 1 | tf_op jit(solution)/shard_map/finish/pallas_call | solution.py:364
  143.9 0.7 broadcast_in_dim.32
  144.5 28.1 %all-to-all-start = ((f32[128,1,128]{2,1,0:T(1,128)}), f32[128,1,128]{2,1,0:T(1,128)S(1)}, u32[]{:S(2)}, u32[]{:S(2)}) async-start(f32[128,1,128]{2,1,0:T(1,128)} %broadcast_in_dim.32), calls=%async_computation | async-start | bytes 131072 | tf_op jit(solution)/shard_map/all_to_all | solution.py:533
  172.6 2.9 %fusion.2.refs_5_ = f32[256,768]{1,0:T(8,128)S(1)} fusion(bf16[768,2048]{1,0:T(8,128)(2,1)} %collective-permute-done.15.refs_0_, pred[256]{0:T(512)(128)(4,1)S(1)} %add_compare_fusion, bf16[1,256,2048]{2,1,0:T(8,128)(2,1)S(1)} %copy-done.1), kind=kOutput, calls=%fused_computation.5 | convolution fusion | flops 805830656 | bytes 4980992 | tf_op jit(solution)/shard_map/dot_general | solution.py:525
  175.5 1.6 collective-permute-start.16
  177.1 2.9 %collective-permute-start.17 = (bf16[192,1024]{1,0:T(8,128)(2,1)S(1)}, bf16[192,1024]{1,0:T(8,128)(2,1)S(1)}, u32[]{:S(2)}, u32[]{:S(2)}) collective-permute-start(bf16[192,1024]{1,0:T(8,128)(2,1)S(1)} %add.146.refs_0_), channel_id=1, source_target_pairs={{0,64},{16,80},{32,96},{48,112},{64,0},{80,16},{96,32},{112,48},{1... | collective-permute-start | bytes 1179656 | tf_op jit(solution)/shard_map/ppermute | solution.py:508
  180.0 0.9 collective-permute-start.18
  181.0 1.2 all-to-all-done
  182.1 0.6 slice_reduce_fusion
  184.9 0.6 multiply_reduce_fusion
  186.2 0.6 gather_fusion
  186.9 0.9 collective-permute-done.16.refs_1_
  187.7 9.9 %collective-permute-done.17.refs_2_ = bf16[192,1024]{1,0:T(8,128)(2,1)S(1)} collective-permute-done((bf16[192,1024]{1,0:T(8,128)(2,1)S(1)}, bf16[192,1024]{1,0:T(8,128)(2,1)S(1)}, u32[]{:S(2)}, u32[]{:S(2)}) %collective-permute-start.17) | collective-permute-done | bytes 393248 | tf_op jit(solution)/shard_map/ppermute | solution.py:508
  197.6 0.9 combine.1.refs_0_
  198.6 2.6 %collective-permute-start.19 = (bf16[192,1024]{1,0:T(8,128)(2,1)S(1)}, bf16[192,1024]{1,0:T(8,128)(2,1)S(1)}, u32[]{:S(2)}, u32[]{:S(2)}) collective-permute-start(bf16[192,1024]{1,0:T(8,128)(2,1)S(1)} %combine.1.refs_0_), channel_id=1, source_target_pairs={{0,16},{16,0},{32,48},{48,32},{64,80},{80,64},{96,112},{112,96},{1... | collective-permute-start | bytes 1179656 | tf_op jit(solution)/shard_map/ppermute | solution.py:547
  201.2 8.5 %collective-permute-done.19.refs_1_ = bf16[192,1024]{1,0:T(8,128)(2,1)S(1)} collective-permute-done((bf16[192,1024]{1,0:T(8,128)(2,1)S(1)}, bf16[192,1024]{1,0:T(8,128)(2,1)S(1)}, u32[]{:S(2)}, u32[]{:S(2)}) %collective-permute-start.19) | collective-permute-done | bytes 393248 | tf_op jit(solution)/shard_map/ppermute | solution.py:547
  209.7 0.6 add.147.refs_0_
  210.3 0.9 collective-permute-start.21
  211.2 1.8 collective-permute-start.23
  213.1 1.1 collective-permute-start.25
  214.2 3.0 %collective-permute-start.20 = (bf16[192,1024]{1,0:T(8,128)(2,1)S(1)}, bf16[192,1024]{1,0:T(8,128)(2,1)S(1)}, u32[]{:S(2)}, u32[]{:S(2)}) collective-permute-start(bf16[192,1024]{1,0:T(8,128)(2,1)S(1)} %add.147.refs_0_), channel_id=1, source_target_pairs={{0,1},{1,0},{2,3},{3,2},{4,5},{5,4},{6,7},{7,6},{8,9},{9,8},{10,11... | collective-permute-start | bytes 1179656 | tf_op jit(solution)/shard_map/ppermute | solution.py:554
  217.1 3.1 %collective-permute-done.21.refs_2_ = bf16[192,1024]{1,0:T(8,128)(2,1)S(1)} collective-permute-done((bf16[192,1024]{1,0:T(8,128)(2,1)S(1)}, bf16[192,1024]{1,0:T(8,128)(2,1)S(1)}, u32[]{:S(2)}, u32[]{:S(2)}) %collective-permute-start.21) | collective-permute-done | bytes 393248 | tf_op jit(solution)/shard_map/ppermute | solution.py:411
  220.2 5.0 %collective-permute-start.22 = (bf16[192,1024]{1,0:T(8,128)(2,1)S(1)}, bf16[192,1024]{1,0:T(8,128)(2,1)}, u32[]{:S(2)}, u32[]{:S(2)}) collective-permute-start(bf16[192,1024]{1,0:T(8,128)(2,1)S(1)} %collective-permute-done.21.refs_2_), channel_id=1, source_target_pairs={{0,1},{1,0},{2,3},{3,2},{4,5},{5,4},{6,7},{7,6},{8,9},{9,8},{10,11... | collective-permute-start | bytes 1179656 | tf_op jit(solution)/shard_map/ppermute | solution.py:554
  225.2 5.6 %collective-permute-start.24 = (bf16[192,1024]{1,0:T(8,128)(2,1)S(1)}, bf16[192,1024]{1,0:T(8,128)(2,1)}, u32[]{:S(2)}, u32[]{:S(2)}) collective-permute-start(bf16[192,1024]{1,0:T(8,128)(2,1)S(1)} %collective-permute-done.23.refs_4_), channel_id=1, source_target_pairs={{0,1},{1,0},{2,3},{3,2},{4,5},{5,4},{6,7},{7,6},{8,9},{9,8},{10,11... | collective-permute-start | bytes 1179656 | tf_op jit(solution)/shard_map/ppermute | solution.py:554
  230.9 1.2 collective-permute-start.26
  232.2 0.6 dynamic_slice.3
  232.8 1.7 fusion.1
  234.5 5.9 %place.1 = f32[768,2048]{1,0:T(8,128)} custom-call(s32[5]{0:T(128)S(1)} %stack.99.info_ref, bf16[192,1024]{1,0:T(8,128)(2,1)S(1)} %add.147.refs_0_, bf16[192,1024]{1,0:T(8,128)(2,1)S(1)} %collective-permute-done.20.refs_1_, bf16[192,1024]{1,0:T(8,128)(2,1)S(1)} %collective-permute-done.21.refs_2_, bf16[192,1024]{1,0:T(8,128)(2,1)} %collective-permute-done.22.refs_3_, ...), custom_call_target="tpu_custom_call" | custom-call | flops 1 | bytes 1 | tf_op jit(solution)/shard_map/place/pallas_call | solution.py:125
  (50 shorter events, 1.0 us)
Async XLA Ops:
  1.4 2.8 %copy-start = (bf16[1,256,2048]{2,1,0:T(8,128)(2,1)S(1)}, bf16[1,256,2048]{2,1,0:T(8,128)(2,1)}, u32[]{:S(2)}) copy-start(bf16[1,256,2048]{2,1,0:T(8,128)(2,1)} %param.16) | copy-start | bytes 3145732
  1.4 1.1 copy-start.3
  2.5 1.0 copy-start.4
  3.6 1.1 copy-start.6
  4.7 17.0 %copy-start.2 = (bf16[1,256,5120]{2,1,0:T(8,128)(2,1)S(1)}, bf16[1,256,5120]{2,1,0:T(8,128)(2,1)}, u32[]{:S(2)}) copy-start(bf16[1,256,5120]{2,1,0:T(8,128)(2,1)} %param.9) | copy-start | bytes 7864324
  9.2 37.1 %collective-permute-start.9 = (bf16[1536,1024]{1,0:T(8,128)(2,1)}, bf16[1536,1024]{1,0:T(8,128)(2,1)}, u32[]{:S(2)}, u32[]{:S(2)}) collective-permute-start(bf16[1536,1024]{1,0:T(8,128)(2,1)} %get-tuple-element.21.refs_0_), channel_id=1, source_target_pairs={{0,1},{1,0},{2,3},{3,2},{4,5},{5,4},{6,7},{7,6},{8,9},{9,8},{10,11... | collective-permute-start | bytes 9437192 | tf_op jit(solution)/shard_map/ppermute | solution.py:461
  10.6 5.9 %collective-permute-start.1 = (bf16[2,256,512]{2,1,0:T(8,128)(2,1)S(1)}, bf16[2,256,512]{2,1,0:T(8,128)(2,1)S(1)}, u32[]{:S(2)}, u32[]{:S(2)}) collective-permute-start(bf16[2,256,512]{2,1,0:T(8,128)(2,1)S(1)} %get-tuple-element.22), channel_id=1, source_target_pairs={{0,1},{1,0},{2,3},{3,2},{4,5},{5,4},{6,7},{7,6},{8,9},{9,8},{10,11... | collective-permute-start | bytes 1572872 | tf_op jit(solution)/shard_map/ppermute | solution.py:425
  17.4 26.0 %collective-permute-start.2 = (bf16[2,512,512]{2,1,0:T(8,128)(2,1)}, bf16[2,512,512]{2,1,0:T(8,128)(2,1)}, u32[]{:S(2)}, u32[]{:S(2)}) collective-permute-start(bf16[2,512,512]{2,1,0:T(8,128)(2,1)} %constant_dynamic-update-slice_fusion.refs_8_.refs_9_), channel_id=1, source_target_pairs={{0,8},{1,9},{2,10},{3,11},{4,12},{5,13},{6,14},{7,15},{16,24},{17,... | collective-permute-start | bytes 3145736 | tf_op jit(solution)/shard_map/ppermute | solution.py:434
  23.4 30.1 %collective-permute-start = (bf16[256,2560]{1,0:T(8,128)(2,1)}, bf16[256,2560]{1,0:T(8,128)(2,1)}, u32[]{:S(2)}, u32[]{:S(2)}) collective-permute-start(bf16[256,2560]{1,0:T(8,128)(2,1)} %pick.2), channel_id=1, source_target_pairs={{0,1},{1,0},{2,3},{3,2},{4,5},{5,4},{6,7},{7,6},{8,9},{9,8},{10,11... | collective-permute-start | bytes 3932168 | tf_op jit(solution)/shard_map/ppermute | solution.py:431
  23.8 30.4 %collective-permute-start.6 = (bf16[2,512,512]{2,1,0:T(8,128)(2,1)}, bf16[2,512,512]{2,1,0:T(8,128)(2,1)}, u32[]{:S(2)}, u32[]{:S(2)}) collective-permute-start(bf16[2,512,512]{2,1,0:T(8,128)(2,1)} %constant_dynamic-update-slice_fusion.refs_8_.refs_9_), channel_id=1, source_target_pairs={{0,2},{1,3},{2,4},{3,5},{4,6},{5,7},{6,0},{7,1},{8,10},{9,11},{10,... | collective-permute-start | bytes 3145736 | tf_op jit(solution)/shard_map/ppermute | solution.py:411
  25.1 30.0 %collective-permute-start.7 = (bf16[2,512,512]{2,1,0:T(8,128)(2,1)}, bf16[2,512,512]{2,1,0:T(8,128)(2,1)}, u32[]{:S(2)}, u32[]{:S(2)}) collective-permute-start(bf16[2,512,512]{2,1,0:T(8,128)(2,1)} %constant_dynamic-update-slice_fusion.refs_8_.refs_9_), channel_id=1, source_target_pairs={{0,6},{1,7},{2,0},{3,1},{4,2},{5,3},{6,4},{7,5},{8,14},{9,15},{10,... | collective-permute-start | bytes 3145736 | tf_op jit(solution)/shard_map/ppermute | solution.py:411
  43.4 30.2 %collective-permute-start.8 = (bf16[2,512,512]{2,1,0:T(8,128)(2,1)}, bf16[2,512,512]{2,1,0:T(8,128)(2,1)}, u32[]{:S(2)}, u32[]{:S(2)}) collective-permute-start(bf16[2,512,512]{2,1,0:T(8,128)(2,1)} %constant_dynamic-update-slice_fusion.refs_8_.refs_9_), channel_id=1, source_target_pairs={{0,4},{1,5},{2,6},{3,7},{4,0},{5,1},{6,2},{7,3},{8,12},{9,13},{10,... | collective-permute-start | bytes 3145736 | tf_op jit(solution)/shard_map/ppermute | solution.py:411
  46.3 93.3 %collective-permute-start.15 = (bf16[768,2048]{1,0:T(8,128)(2,1)}, bf16[768,2048]{1,0:T(8,128)(2,1)}, u32[]{:S(2)}, u32[]{:S(2)}) collective-permute-start(bf16[768,2048]{1,0:T(8,128)(2,1)} %param.17), channel_id=1, source_target_pairs={{0,24},{8,16},{16,8},{24,0},{32,56},{40,48},{48,40},{56,32},{64,88... | collective-permute-start | bytes 9437192 | tf_op jit(solution)/shard_map/ppermute | solution.py:444
  53.5 57.6 %collective-permute-start.3 = (bf16[2,512,512]{2,1,0:T(8,128)(2,1)}, bf16[2,512,512]{2,1,0:T(8,128)(2,1)S(1)}, u32[]{:S(2)}, u32[]{:S(2)}) collective-permute-start(bf16[2,512,512]{2,1,0:T(8,128)(2,1)} %collective-permute-done.2.refs_4_.refs_0_.refs_1_), channel_id=1, source_target_pairs={{8,10},{9,11},{10,12},{11,13},{12,14},{13,15},{14,8},{15,9},{24,26... | collective-permute-start | bytes 3145736 | tf_op jit(solution)/shard_map/ppermute | solution.py:411
  54.3 61.3 %collective-permute-start.4 = (bf16[2,512,512]{2,1,0:T(8,128)(2,1)}, bf16[2,512,512]{2,1,0:T(8,128)(2,1)S(1)}, u32[]{:S(2)}, u32[]{:S(2)}) collective-permute-start(bf16[2,512,512]{2,1,0:T(8,128)(2,1)} %collective-permute-done.2.refs_4_.refs_0_.refs_1_), channel_id=1, source_target_pairs={{8,14},{9,15},{10,8},{11,9},{12,10},{13,11},{14,12},{15,13},{24,30... | collective-permute-start | bytes 3145736 | tf_op jit(solution)/shard_map/ppermute | solution.py:411
  55.0 60.6 %collective-permute-start.5 = (bf16[2,512,512]{2,1,0:T(8,128)(2,1)}, bf16[2,512,512]{2,1,0:T(8,128)(2,1)S(1)}, u32[]{:S(2)}, u32[]{:S(2)}) collective-permute-start(bf16[2,512,512]{2,1,0:T(8,128)(2,1)} %collective-permute-done.2.refs_4_.refs_0_.refs_1_), channel_id=1, source_target_pairs={{8,12},{9,13},{10,14},{11,15},{12,8},{13,9},{14,10},{15,11},{24,28... | collective-permute-start | bytes 3145736 | tf_op jit(solution)/shard_map/ppermute | solution.py:411
  73.5 35.2 %collective-permute-start.10 = (bf16[768,1024]{1,0:T(8,128)(2,1)S(1)}, bf16[768,1024]{1,0:T(8,128)(2,1)S(1)}, u32[]{:S(2)}, u32[]{:S(2)}) collective-permute-start(bf16[768,1024]{1,0:T(8,128)(2,1)S(1)} %get-tuple-element.24.refs_10_), channel_id=1, source_target_pairs={{0,8},{8,0},{1,9},{9,1},{2,10},{10,2},{3,11},{11,3},{4,12},{12,4},... | collective-permute-start | bytes 4718600 | tf_op jit(solution)/shard_map/ppermute | solution.py:472
  108.7 1.2 copy-start.5
  110.9 15.0 %collective-permute-start.11 = (bf16[192,1024]{1,0:T(8,128)(2,1)S(1)}, bf16[192,1024]{1,0:T(8,128)(2,1)S(1)}, u32[]{:S(2)}, u32[]{:S(2)}) collective-permute-start(bf16[192,1024]{1,0:T(8,128)(2,1)S(1)} %get-tuple-element.31), channel_id=1, source_target_pairs={{0,2},{1,3},{2,4},{3,5},{4,6},{5,7},{6,0},{7,1},{8,10},{9,11},{10,... | collective-permute-start | bytes 1179656 | tf_op jit(solution)/shard_map/ppermute | solution.py:411
  111.1 4.5 %copy-start.9 = (bf16[2,512,512]{2,1,0:T(8,128)(2,1)}, bf16[2,512,512]{2,1,0:T(8,128)(2,1)S(1)}, u32[]{:S(2)}) copy-start(bf16[2,512,512]{2,1,0:T(8,128)(2,1)S(1)} %collective-permute-done.3.refs_0_.refs_1_) | copy-start | bytes 3145732
  111.1 19.5 %collective-permute-start.12 = (bf16[192,1024]{1,0:T(8,128)(2,1)S(1)}, bf16[192,1024]{1,0:T(8,128)(2,1)S(1)}, u32[]{:S(2)}, u32[]{:S(2)}) collective-permute-start(bf16[192,1024]{1,0:T(8,128)(2,1)S(1)} %get-tuple-element.32), channel_id=1, source_target_pairs={{0,4},{1,5},{2,6},{3,7},{4,0},{5,1},{6,2},{7,3},{8,12},{9,13},{10,... | collective-permute-start | bytes 1179656 | tf_op jit(solution)/shard_map/ppermute | solution.py:411
  115.6 1.0 copy-start.10
  115.6 16.5 %collective-permute-start.13 = (bf16[192,1024]{1,0:T(8,128)(2,1)S(1)}, bf16[192,1024]{1,0:T(8,128)(2,1)S(1)}, u32[]{:S(2)}, u32[]{:S(2)}) collective-permute-start(bf16[192,1024]{1,0:T(8,128)(2,1)S(1)} %get-tuple-element.33), channel_id=1, source_target_pairs={{0,6},{1,7},{2,0},{3,1},{4,2},{5,3},{6,4},{7,5},{8,14},{9,15},{10,... | collective-permute-start | bytes 1179656 | tf_op jit(solution)/shard_map/ppermute | solution.py:411
  115.6 1.3 copy-start.11
  132.8 3.9 %copy-start.1 = (bf16[1,256,2048]{2,1,0:T(8,128)(2,1)S(1)}, bf16[1,256,2048]{2,1,0:T(8,128)(2,1)}, u32[]{:S(2)}) copy-start(bf16[1,256,2048]{2,1,0:T(8,128)(2,1)} %param.16) | copy-start | bytes 3145732
  134.5 5.2 %collective-permute-start.14 = (bf16[256,2560]{1,0:T(8,128)(2,1)}, bf16[256,2560]{1,0:T(8,128)(2,1)}, u32[]{:S(2)}, u32[]{:S(2)}) collective-permute-start(bf16[256,2560]{1,0:T(8,128)(2,1)} %pick.3), channel_id=1, source_target_pairs={{0,1},{1,0},{2,3},{3,2},{4,5},{5,4},{6,7},{7,6},{8,9},{9,8},{10,11... | collective-permute-start | bytes 3932168 | tf_op jit(solution)/shard_map/ppermute | solution.py:515
  136.7 3.0 %copy-start.7 = (f32[5120]{0:T(1024)S(1)}, f32[5120]{0:T(1024)}, u32[]{:S(2)}) copy-start(f32[5120]{0:T(1024)} %param.13) | copy-start | bytes 61444
  136.7 3.0 %copy-start.8 = (f32[5120]{0:T(1024)S(1)}, f32[5120]{0:T(1024)}, u32[]{:S(2)}) copy-start(f32[5120]{0:T(1024)} %param.14) | copy-start | bytes 61444
  144.5 37.6 %all-to-all-start = ((f32[128,1,128]{2,1,0:T(1,128)}), f32[128,1,128]{2,1,0:T(1,128)S(1)}, u32[]{:S(2)}, u32[]{:S(2)}) async-start(f32[128,1,128]{2,1,0:T(1,128)} %broadcast_in_dim.32), calls=%async_computation | async-start | bytes 131072 | tf_op jit(solution)/shard_map/all_to_all | solution.py:533
  175.5 12.2 %collective-permute-start.16 = (bf16[192,1024]{1,0:T(8,128)(2,1)S(1)}, bf16[192,1024]{1,0:T(8,128)(2,1)S(1)}, u32[]{:S(2)}, u32[]{:S(2)}) collective-permute-start(bf16[192,1024]{1,0:T(8,128)(2,1)S(1)} %add.146.refs_0_), channel_id=1, source_target_pairs={{0,32},{16,48},{32,64},{48,80},{64,96},{80,112},{96,0},{112,16},{1... | collective-permute-start | bytes 1179656 | tf_op jit(solution)/shard_map/ppermute | solution.py:508
  177.1 20.5 %collective-permute-start.17 = (bf16[192,1024]{1,0:T(8,128)(2,1)S(1)}, bf16[192,1024]{1,0:T(8,128)(2,1)S(1)}, u32[]{:S(2)}, u32[]{:S(2)}) collective-permute-start(bf16[192,1024]{1,0:T(8,128)(2,1)S(1)} %add.146.refs_0_), channel_id=1, source_target_pairs={{0,64},{16,80},{32,96},{48,112},{64,0},{80,16},{96,32},{112,48},{1... | collective-permute-start | bytes 1179656 | tf_op jit(solution)/shard_map/ppermute | solution.py:508
  180.0 17.6 %collective-permute-start.18 = (bf16[192,1024]{1,0:T(8,128)(2,1)S(1)}, bf16[192,1024]{1,0:T(8,128)(2,1)S(1)}, u32[]{:S(2)}, u32[]{:S(2)}) collective-permute-start(bf16[192,1024]{1,0:T(8,128)(2,1)S(1)} %add.146.refs_0_), channel_id=1, source_target_pairs={{0,96},{16,112},{32,0},{48,16},{64,32},{80,48},{96,64},{112,80},{1... | collective-permute-start | bytes 1179656 | tf_op jit(solution)/shard_map/ppermute | solution.py:508
  198.6 11.1 %collective-permute-start.19 = (bf16[192,1024]{1,0:T(8,128)(2,1)S(1)}, bf16[192,1024]{1,0:T(8,128)(2,1)S(1)}, u32[]{:S(2)}, u32[]{:S(2)}) collective-permute-start(bf16[192,1024]{1,0:T(8,128)(2,1)S(1)} %combine.1.refs_0_), channel_id=1, source_target_pairs={{0,16},{16,0},{32,48},{48,32},{64,80},{80,64},{96,112},{112,96},{1... | collective-permute-start | bytes 1179656 | tf_op jit(solution)/shard_map/ppermute | solution.py:547
  210.3 9.9 %collective-permute-start.21 = (bf16[192,1024]{1,0:T(8,128)(2,1)S(1)}, bf16[192,1024]{1,0:T(8,128)(2,1)S(1)}, u32[]{:S(2)}, u32[]{:S(2)}) collective-permute-start(bf16[192,1024]{1,0:T(8,128)(2,1)S(1)} %add.147.refs_0_), channel_id=1, source_target_pairs={{0,2},{1,3},{2,4},{3,5},{4,6},{5,7},{6,0},{7,1},{8,10},{9,11},{10,... | collective-permute-start | bytes 1179656 | tf_op jit(solution)/shard_map/ppermute | solution.py:411
  211.2 14.0 %collective-permute-start.23 = (bf16[192,1024]{1,0:T(8,128)(2,1)S(1)}, bf16[192,1024]{1,0:T(8,128)(2,1)S(1)}, u32[]{:S(2)}, u32[]{:S(2)}) collective-permute-start(bf16[192,1024]{1,0:T(8,128)(2,1)S(1)} %add.147.refs_0_), channel_id=1, source_target_pairs={{0,6},{1,7},{2,0},{3,1},{4,2},{5,3},{6,4},{7,5},{8,14},{9,15},{10,... | collective-permute-start | bytes 1179656 | tf_op jit(solution)/shard_map/ppermute | solution.py:411
  213.1 17.8 %collective-permute-start.25 = (bf16[192,1024]{1,0:T(8,128)(2,1)S(1)}, bf16[192,1024]{1,0:T(8,128)(2,1)S(1)}, u32[]{:S(2)}, u32[]{:S(2)}) collective-permute-start(bf16[192,1024]{1,0:T(8,128)(2,1)S(1)} %add.147.refs_0_), channel_id=1, source_target_pairs={{0,4},{1,5},{2,6},{3,7},{4,0},{5,1},{6,2},{7,3},{8,12},{9,13},{10,... | collective-permute-start | bytes 1179656 | tf_op jit(solution)/shard_map/ppermute | solution.py:411
  214.2 20.3 %collective-permute-start.20 = (bf16[192,1024]{1,0:T(8,128)(2,1)S(1)}, bf16[192,1024]{1,0:T(8,128)(2,1)S(1)}, u32[]{:S(2)}, u32[]{:S(2)}) collective-permute-start(bf16[192,1024]{1,0:T(8,128)(2,1)S(1)} %add.147.refs_0_), channel_id=1, source_target_pairs={{0,1},{1,0},{2,3},{3,2},{4,5},{5,4},{6,7},{7,6},{8,9},{9,8},{10,11... | collective-permute-start | bytes 1179656 | tf_op jit(solution)/shard_map/ppermute | solution.py:554
  220.2 14.2 %collective-permute-start.22 = (bf16[192,1024]{1,0:T(8,128)(2,1)S(1)}, bf16[192,1024]{1,0:T(8,128)(2,1)}, u32[]{:S(2)}, u32[]{:S(2)}) collective-permute-start(bf16[192,1024]{1,0:T(8,128)(2,1)S(1)} %collective-permute-done.21.refs_2_), channel_id=1, source_target_pairs={{0,1},{1,0},{2,3},{3,2},{4,5},{5,4},{6,7},{7,6},{8,9},{9,8},{10,11... | collective-permute-start | bytes 1179656 | tf_op jit(solution)/shard_map/ppermute | solution.py:554
  225.2 9.2 %collective-permute-start.24 = (bf16[192,1024]{1,0:T(8,128)(2,1)S(1)}, bf16[192,1024]{1,0:T(8,128)(2,1)}, u32[]{:S(2)}, u32[]{:S(2)}) collective-permute-start(bf16[192,1024]{1,0:T(8,128)(2,1)S(1)} %collective-permute-done.23.refs_4_), channel_id=1, source_target_pairs={{0,1},{1,0},{2,3},{3,2},{4,5},{5,4},{6,7},{7,6},{8,9},{9,8},{10,11... | collective-permute-start | bytes 1179656 | tf_op jit(solution)/shard_map/ppermute | solution.py:554
  230.9 3.6 %collective-permute-start.26 = (bf16[192,1024]{1,0:T(8,128)(2,1)S(1)}, bf16[192,1024]{1,0:T(8,128)(2,1)}, u32[]{:S(2)}, u32[]{:S(2)}) collective-permute-start(bf16[192,1024]{1,0:T(8,128)(2,1)S(1)} %collective-permute-done.25.refs_6_), channel_id=1, source_target_pairs={{0,1},{1,0},{2,3},{3,2},{4,5},{5,4},{6,7},{7,6},{8,9},{9,8},{10,11... | collective-permute-start | bytes 1179656 | tf_op jit(solution)/shard_map/ppermute | solution.py:554
where the time goes:
time: 241 us; the launch traced here: 240 us
  waiting for transfers between devices  88.5 us (37%)
  starting transfers between devices  79 us (33%)
  Pallas kernels  50.4 us (21%)
  local copies, waits for them, and re-layouts  9.24 us (4%)
  matrix products  5.83 us (2%)
  between operations  4.31 us (2%)
  other arithmetic  3.15 us (1%)
    all_to_all x1, starting transfers between devices, shards(): lax.all_to_all(jnp.broadcast_to(partial, (n_dev, HEAD_DIM)), ('replica',...  28.1 us
    ppermute x12, waiting for transfers between devices, move(): return lax.ppermute(array, ('fsdp', 'context'), along_x(step, planes))  27.1 us
    pallas_call x2, Pallas kernels, attend(): pl.pallas_call(kernel, grid_spec=pltpu.PrefetchScalarGridSpec(num_scalar_...  25.1 us
    ppermute x1, waiting for transfers between devices, shards(): got = lax.ppermute(p_send, 'fsdp', [(0, 1), (1, 0)])  19 us
    ppermute x1, waiting for transfers between devices, shards(): cross = {0: lax.ppermute(kv_own, 'fsdp', [(0, 1)])}  16.9 us
    ppermute x12, starting transfers between devices, move(): return lax.ppermute(array, ('fsdp', 'context'), along_x(step, planes))  16.2 us
    ppermute x4, starting transfers between devices, shards(): parts += [part, lax.ppermute(part, 'context', swap)]  14.8 us
    ppermute x3, waiting for transfers between devices, along_z(): return lax.ppermute(array, 'replica', pairs) if dz else array  10.8 us
  transfers between devices with their start and end apart: 28, of which 11 were waited for; matrix products, arithmetic and copies ran while one was open for 5% of the time, Pallas kernels for 14%

commit v1 on v0

--- a/solution.py
+++ b/solution.py
@@ -471,13 +471,23 @@
     )
     got = lax.ppermute(p_send, "fsdp", [(0, 1), (1, 0)])
 
+    valid = tok_base + jnp.arange(rows, dtype=jnp.int32) < length
+    masked = jnp.where(valid[:, None], cotangent[0], jnp.zeros_like(cotangent[0]))
+
+    def raw(weight):
+        return lax.dot_general(
+            masked, weight, (((1,), (1,)), ((), ())), preferred_element_type=F32
+        )
+
+    raw_own = raw(qkv_weight)
+
     state = step(
         other(0) + near(1, 3, 2, 0),
         [cross[0], ring[1], ring[3], ring[2], kv_own],
         [(0, 2), (2, 2)],
         (),
         flops=24 * 10**9,
-        after=(p_send,),
+        after=(p_send, raw_own),
     )
     chunks = add(
         tok_info,
@@ -518,15 +528,7 @@
         (weight_other,),
     )
 
-    valid = tok_base + jnp.arange(rows, dtype=jnp.int32) < length
-    masked = jnp.where(valid[:, None], cotangent[0], jnp.zeros_like(cotangent[0]))
-
-    def raw(weight):
-        return lax.dot_general(
-            masked, weight, (((1,), (1,)), ((), ())), preferred_element_type=F32
-        )
-
-    raw_own, raw_other = raw(qkv_weight), raw(weight_other)
+    raw_other = raw(weight_other)
 
     partial = reward_sum[:1] / jnp.sqrt(length.astype(F32))
     n_dev = n_rep * n_fsdp * n_ctx

time: 241 us -> 240 us (level)
  waiting for transfers between devices: 88.5 us -> 85.1 us
    ppermute x12, waiting for transfers between devices: 27.1 us -> 21.4 us  [move(): return lax.ppermute(array, ('fsdp', 'context'), along_x(step, planes))]
    ppermute x1, waiting for transfers between devices: 0.01 us -> 2.84 us  [shards(): lax.ppermute(mixed_there, 'context', swap)]
    unnamed x25 -> x33, local copies, waits for them, and re-layouts: 6.08 us -> 7.13 us
  transfers between devices with their start and end apart: 28 -> 28, of which waited for: 11 -> 12; matrix products, arithmetic and copies ran while one was open for 5% -> 6% of each run, Pallas kernels for 14% -> 14%
where the time goes in v1:
time: 240 us; the launch traced here: 239 us
  waiting for transfers between devices  85.1 us (35%)
  starting transfers between devices  78.4 us (33%)
  Pallas kernels  50.3 us (21%)
  local copies, waits for them, and re-layouts  10.3 us (4%)
  matrix products  6.3 us (3%)
  between operations  4.35 us (2%)
  other arithmetic  4.07 us (2%)
    all_to_all x1, starting transfers between devices, shards(): lax.all_to_all(jnp.broadcast_to(partial, (n_dev, HEAD_DIM)), ('replica',...  26.2 us
    pallas_call x2, Pallas kernels, attend(): pl.pallas_call(kernel, grid_spec=pltpu.PrefetchScalarGridSpec(num_scalar_...  25.1 us
    ppermute x12, waiting for transfers between devices, move(): return lax.ppermute(array, ('fsdp', 'context'), along_x(step, planes))  21.4 us
    ppermute x1, waiting for transfers between devices, shards(): got = lax.ppermute(p_send, 'fsdp', [(0, 1), (1, 0)])  18.7 us
    ppermute x1, waiting for transfers between devices, shards(): cross = {0: lax.ppermute(kv_own, 'fsdp', [(0, 1)])}  17.8 us
    ppermute x12, starting transfers between devices, move(): return lax.ppermute(array, ('fsdp', 'context'), along_x(step, planes))  17.7 us
    ppermute x4, starting transfers between devices, shards(): parts += [part, lax.ppermute(part, 'context', swap)]  15.1 us
    ppermute x3, waiting for transfers between devices, along_z(): return lax.ppermute(array, 'replica', pairs) if dz else array  10.2 us
  transfers between devices with their start and end apart: 28, of which 12 were waited for; matrix products, arithmetic and copies ran while one was open for 6% of the time, Pallas kernels for 14%

profile of v1, /device:TPU:1, one launch (start us, length us, event | category | flops | bytes accessed | tf_op | source)
XLA Modules:
  0.0 238.9 jit_solution(6952224459612027785)
XLA Ops:
  1.4 1.1 copy-done.5
  2.5 1.0 copy-done.6
  3.6 0.6 split_kv.1
  4.2 0.5 copy-done.10
  4.7 4.5 %policy_terms.1 = (bf16[1536,1024]{1,0:T(8,128)(2,1)}, bf16[1536,1024]{1,0:T(8,128)(2,1)S(1)}) custom-call(s32[5]{0:T(128)S(1)} %stack.84.info_ref, bf16[256,1536]{1,0:T(8,128)(2,1)S(1)} %bitcast.60, bf16[256,2048]{1,0:T(8,128)(2,1)S(1)} %bitcast.49, bf16[256,2048]{1,0:T(8,128)(2,1)S(1)} %bitcast.50, bf16[2,256,512]{2,1,0:T(8,128)(2,1)S(1)} %get-tuple-element.20.refs_0_), custom_call_target="tpu_custom_call" | custom-call | flops 1 | bytes 1 | tf_op jit(solution)/shard_map/policy_terms/pallas_call | solution.py:68
  9.2 1.4 collective-permute-start.9
  10.7 0.9 constant_dynamic-update-slice_fusion.1
  11.5 5.0 %collective-permute-done.1 = bf16[2,256,512]{2,1,0:T(8,128)(2,1)S(1)} collective-permute-done((bf16[2,256,512]{2,1,0:T(8,128)(2,1)S(1)}, bf16[2,256,512]{2,1,0:T(8,128)(2,1)S(1)}, u32[]{:S(2)}, u32[]{:S(2)}) %collective-permute-start.1) | collective-permute-done | bytes 524320 | tf_op jit(solution)/shard_map/ppermute | solution.py:425
  16.6 0.9 constant_dynamic-update-slice_fusion.refs_8_.refs_9_
  17.4 3.3 %collective-permute-start.2 = (bf16[2,512,512]{2,1,0:T(8,128)(2,1)}, bf16[2,512,512]{2,1,0:T(8,128)(2,1)S(1)}, u32[]{:S(2)}, u32[]{:S(2)}) collective-permute-start(bf16[2,512,512]{2,1,0:T(8,128)(2,1)} %constant_dynamic-update-slice_fusion.refs_8_.refs_9_), channel_id=1, source_target_pairs={{0,8},{1,9},{2,10},{3,11},{4,12},{5,13},{6,14},{7,15},{16,24},{17,... | collective-permute-start | bytes 3145736 | tf_op jit(solution)/shard_map/ppermute | solution.py:434
  20.8 1.7 pick.2
  22.9 1.2 collective-permute-start.6
  24.1 1.5 collective-permute-start.7
  25.6 17.8 %collective-permute-done.2.refs_4_.refs_0_.refs_1_ = bf16[2,512,512]{2,1,0:T(8,128)(2,1)S(1)} collective-permute-done((bf16[2,512,512]{2,1,0:T(8,128)(2,1)}, bf16[2,512,512]{2,1,0:T(8,128)(2,1)S(1)}, u32[]{:S(2)}, u32[]{:S(2)}) %collective-permute-start.2) | collective-permute-done | bytes 1048608 | tf_op jit(solution)/shard_map/ppermute | solution.py:434
  43.4 1.0 copy-done.7
  44.5 2.7 %collective-permute-start.8 = (bf16[2,512,512]{2,1,0:T(8,128)(2,1)}, bf16[2,512,512]{2,1,0:T(8,128)(2,1)}, u32[]{:S(2)}, u32[]{:S(2)}) collective-permute-start(bf16[2,512,512]{2,1,0:T(8,128)(2,1)} %constant_dynamic-update-slice_fusion.refs_8_.refs_9_), channel_id=1, source_target_pairs={{0,4},{1,5},{2,6},{3,7},{4,0},{5,1},{6,2},{7,3},{8,12},{9,13},{10,... | collective-permute-start | bytes 3145736 | tf_op jit(solution)/shard_map/ppermute | solution.py:411
  47.4 3.3 %fusion.3.refs_11_.refs_4_ = f32[256,768]{1,0:T(8,128)S(1)} fusion(bf16[768,2048]{1,0:T(8,128)(2,1)} %param.17, pred[256]{0:T(512)(128)(4,1)S(1)} %add_compare_fusion, bf16[1,256,2048]{2,1,0:T(8,128)(2,1)} %param.16), kind=kOutput, calls=%fused_computation.6 | convolution fusion | flops 805830656 | bytes 4980992 | tf_op jit(solution)/shard_map/dot_general | solution.py:478
  50.7 3.7 %collective-permute-start.15 = (bf16[768,2048]{1,0:T(8,128)(2,1)}, bf16[768,2048]{1,0:T(8,128)(2,1)}, u32[]{:S(2)}, u32[]{:S(2)}) collective-permute-start(bf16[768,2048]{1,0:T(8,128)(2,1)} %param.17), channel_id=1, source_target_pairs={{0,24},{8,16},{16,8},{24,0},{32,56},{40,48},{48,40},{56,32},{64,88... | collective-permute-start | bytes 9437192 | tf_op jit(solution)/shard_map/ppermute | solution.py:444
  54.5 3.5 %add.144 = (bf16[768,1024]{1,0:T(8,128)(2,1)S(1)}, bf16[768,1024]{1,0:T(8,128)(2,1)S(1)}) custom-call(s32[5]{0:T(128)S(1)} %stack.84.info_ref, bf16[1536,1024]{1,0:T(8,128)(2,1)S(1)} %get-tuple-element.23.refs_0_.refs_2_, bf16[1536,1024]{1,0:T(8,128)(2,1)} %collective-permute-done.9.refs_1_.refs_3_, ...), custom_call_target="tpu_custom_call" | custom-call | flops 1 | bytes 1 | tf_op jit(solution)/shard_map/add/pallas_call | solution.py:161
  57.9 0.7 collective-permute-start.3
  58.7 0.7 collective-permute-start.4
  59.4 0.7 collective-permute-start.5
  60.2 12.4 %collective-permute-done.8.refs_6_.refs_7_ = bf16[2,512,512]{2,1,0:T(8,128)(2,1)} collective-permute-done((bf16[2,512,512]{2,1,0:T(8,128)(2,1)}, bf16[2,512,512]{2,1,0:T(8,128)(2,1)}, u32[]{:S(2)}, u32[]{:S(2)}) %collective-permute-start.8) | collective-permute-done | bytes 1048608 | tf_op jit(solution)/shard_map/ppermute | solution.py:411
  72.6 16.1 %attend.2 = (f32[4,512,640]{2,1,0:T(8,128)}, f32[4,512,128]{2,1,0:T(8,128)}) custom-call(s32[8]{0:T(128)S(1)} %stack.94.info_ref, bf16[256,5120]{1,0:T(8,128)(2,1)} %bitcast.53, bf16[256,2560]{1,0:T(8,128)(2,1)} %collective-permute-done.got_ref, bf16[2,512,512]{2,1,0:T(8,128)(2,1)} %copy-done.7, bf16[2,512,512]{2,1,0:T(8,128)(2,1)} %copy-done.7, ...), custom_call_target="tpu_custom_call" | custom-call | flops 24000000000 | bytes 1 | tf_op jit(solution)/shard_map/attend/pallas_call | solution.py:317
  88.8 18.7 %collective-permute-done.10.refs_1_.refs_3_.refs_5_.refs_7_ = bf16[768,1024]{1,0:T(8,128)(2,1)S(1)} collective-permute-done((bf16[768,1024]{1,0:T(8,128)(2,1)S(1)}, bf16[768,1024]{1,0:T(8,128)(2,1)S(1)}, u32[]{:S(2)}, u32[]{:S(2)}) %collective-permute-start.10) | collective-permute-done | bytes 1572896 | tf_op jit(solution)/shard_map/ppermute | solution.py:472
  107.5 1.2 copy-done.9
  108.7 0.9 add.145
  109.7 6.0 %collective-permute-start.12 = (bf16[192,1024]{1,0:T(8,128)(2,1)S(1)}, bf16[192,1024]{1,0:T(8,128)(2,1)S(1)}, u32[]{:S(2)}, u32[]{:S(2)}) collective-permute-start(bf16[192,1024]{1,0:T(8,128)(2,1)S(1)} %get-tuple-element.32), channel_id=1, source_target_pairs={{0,4},{1,5},{2,6},{3,7},{4,0},{5,1},{6,2},{7,3},{8,12},{9,13},{10,... | collective-permute-start | bytes 1179656 | tf_op jit(solution)/shard_map/ppermute | solution.py:411
  115.7 0.9 copy-done.14
  117.0 8.9 %attend.3 = (bf16[256,2560]{1,0:T(8,128)(2,1)S(1)}, bf16[256,2560]{1,0:T(8,128)(2,1)S(1)}) custom-call(s32[6]{0:T(128)S(1)} %stack.89.info_ref, bf16[256,5120]{1,0:T(8,128)(2,1)} %bitcast.54, bf16[256,2560]{1,0:T(8,128)(2,1)} %collective-permute-done.got_ref, bf16[2,512,512]{2,1,0:T(8,128)(2,1)} %copy-done.13, bf16[2,512,512]{2,1,0:T(8,128)(2,1)} %copy-done.13, ...), custom_call_target="tpu_custom_call" | custom-call | flops 24000000000 | bytes 1 | tf_op jit(solution)/shard_map/attend/pallas_call | solution.py:317
  126.0 3.9 %collective-permute-done.12.refs_2_ = bf16[192,1024]{1,0:T(8,128)(2,1)S(1)} collective-permute-done((bf16[192,1024]{1,0:T(8,128)(2,1)S(1)}, bf16[192,1024]{1,0:T(8,128)(2,1)S(1)}, u32[]{:S(2)}, u32[]{:S(2)}) %collective-permute-start.12) | collective-permute-done | bytes 393248 | tf_op jit(solution)/shard_map/ppermute | solution.py:411
  129.9 2.2 collective-permute-done.13.refs_3_
  132.1 0.7 add.146.refs_0_
  132.9 1.7 pick.3
  134.6 2.1 collective-permute-start.14
  136.8 2.8 %collective-permute-done.14.other_ref = bf16[256,2560]{1,0:T(8,128)(2,1)} collective-permute-done((bf16[256,2560]{1,0:T(8,128)(2,1)}, bf16[256,2560]{1,0:T(8,128)(2,1)}, u32[]{:S(2)}, u32[]{:S(2)}) %collective-permute-start.14) | collective-permute-done | bytes 1310752 | tf_op jit(solution)/shard_map/ppermute | solution.py:525
  139.7 4.2 %finish.1 = (bf16[256,5120]{1,0:T(8,128)(2,1)}, f32[8,128]{1,0:T(8,128)S(1)}) custom-call(s32[5]{0:T(128)S(1)} %stack.84.info_ref, bf16[256,2560]{1,0:T(8,128)(2,1)S(1)} %get-tuple-element.29.refs_4_.own_ref, bf16[256,2560]{1,0:T(8,128)(2,1)} %collective-permute-done.14.other_ref, f32[1,5120]{1,0:T(1,128)S(1)} %bitcast.61, f32[1,5120]{1,0:T(1,128)S(1)} %bitcast.62, ...), custom_call_target="tpu_custom_call" | custom-call | flops 1 | bytes 1 | tf_op jit(solution)/shard_map/finish/pallas_call | solution.py:364
  143.8 0.7 broadcast_in_dim.34
  144.5 26.2 %all-to-all-start = ((f32[128,1,128]{2,1,0:T(1,128)}), f32[128,1,128]{2,1,0:T(1,128)}, u32[]{:S(2)}, u32[]{:S(2)}) async-start(f32[128,1,128]{2,1,0:T(1,128)} %broadcast_in_dim.34), calls=%async_computation | async-start | bytes 131072 | tf_op jit(solution)/shard_map/all_to_all | solution.py:535
  170.7 3.0 %fusion.2.refs_5_ = f32[256,768]{1,0:T(8,128)S(1)} fusion(bf16[768,2048]{1,0:T(8,128)(2,1)} %collective-permute-done.15.refs_0_, pred[256]{0:T(512)(128)(4,1)S(1)} %add_compare_fusion, bf16[1,256,2048]{2,1,0:T(8,128)(2,1)S(1)} %copy-done.1), kind=kOutput, calls=%fused_computation.5 | convolution fusion | flops 805830656 | bytes 4980992 | tf_op jit(solution)/shard_map/dot_general | solution.py:478
  173.7 1.8 collective-permute-start.16
  175.6 2.9 %collective-permute-start.17 = (bf16[192,1024]{1,0:T(8,128)(2,1)S(1)}, bf16[192,1024]{1,0:T(8,128)(2,1)S(1)}, u32[]{:S(2)}, u32[]{:S(2)}) collective-permute-start(bf16[192,1024]{1,0:T(8,128)(2,1)S(1)} %add.146.refs_0_), channel_id=1, source_target_pairs={{0,64},{16,80},{32,96},{48,112},{64,0},{80,16},{96,32},{112,48},{1... | collective-permute-start | bytes 1179656 | tf_op jit(solution)/shard_map/ppermute | solution.py:518
  178.5 0.9 collective-permute-start.18
  179.4 0.6 all-to-all-done
  180.0 1.5 slice_reduce_fusion
  183.7 0.6 multiply_reduce_fusion
  185.1 0.6 gather_fusion
  185.7 0.6 collective-permute-done.16.refs_1_
  186.3 9.6 %collective-permute-done.17.refs_2_ = bf16[192,1024]{1,0:T(8,128)(2,1)S(1)} collective-permute-done((bf16[192,1024]{1,0:T(8,128)(2,1)S(1)}, bf16[192,1024]{1,0:T(8,128)(2,1)S(1)}, u32[]{:S(2)}, u32[]{:S(2)}) %collective-permute-start.17) | collective-permute-done | bytes 393248 | tf_op jit(solution)/shard_map/ppermute | solution.py:518
  195.9 0.9 combine.1.refs_0_
  196.9 2.8 %collective-permute-start.19 = (bf16[192,1024]{1,0:T(8,128)(2,1)S(1)}, bf16[192,1024]{1,0:T(8,128)(2,1)S(1)}, u32[]{:S(2)}, u32[]{:S(2)}) collective-permute-start(bf16[192,1024]{1,0:T(8,128)(2,1)S(1)} %combine.1.refs_0_), channel_id=1, source_target_pairs={{0,16},{16,0},{32,48},{48,32},{64,80},{80,64},{96,112},{112,96},{1... | collective-permute-start | bytes 1179656 | tf_op jit(solution)/shard_map/ppermute | solution.py:549
  199.6 8.3 %collective-permute-done.19.refs_1_ = bf16[192,1024]{1,0:T(8,128)(2,1)S(1)} collective-permute-done((bf16[192,1024]{1,0:T(8,128)(2,1)S(1)}, bf16[192,1024]{1,0:T(8,128)(2,1)S(1)}, u32[]{:S(2)}, u32[]{:S(2)}) %collective-permute-start.19) | collective-permute-done | bytes 393248 | tf_op jit(solution)/shard_map/ppermute | solution.py:549
  207.9 0.6 add.147.refs_0_
  208.6 1.1 collective-permute-start.21
  209.7 1.7 collective-permute-start.23
  211.3 1.3 collective-permute-start.25
  212.6 3.0 %collective-permute-start.20 = (bf16[192,1024]{1,0:T(8,128)(2,1)S(1)}, bf16[192,1024]{1,0:T(8,128)(2,1)S(1)}, u32[]{:S(2)}, u32[]{:S(2)}) collective-permute-start(bf16[192,1024]{1,0:T(8,128)(2,1)S(1)} %add.147.refs_0_), channel_id=1, source_target_pairs={{0,1},{1,0},{2,3},{3,2},{4,5},{5,4},{6,7},{7,6},{8,9},{9,8},{10,11... | collective-permute-start | bytes 1179656 | tf_op jit(solution)/shard_map/ppermute | solution.py:556
  215.6 2.8 %collective-permute-done.21.refs_2_ = bf16[192,1024]{1,0:T(8,128)(2,1)S(1)} collective-permute-done((bf16[192,1024]{1,0:T(8,128)(2,1)S(1)}, bf16[192,1024]{1,0:T(8,128)(2,1)S(1)}, u32[]{:S(2)}, u32[]{:S(2)}) %collective-permute-start.21) | collective-permute-done | bytes 393248 | tf_op jit(solution)/shard_map/ppermute | solution.py:411
  218.4 4.9 %collective-permute-start.22 = (bf16[192,1024]{1,0:T(8,128)(2,1)S(1)}, bf16[192,1024]{1,0:T(8,128)(2,1)}, u32[]{:S(2)}, u32[]{:S(2)}) collective-permute-start(bf16[192,1024]{1,0:T(8,128)(2,1)S(1)} %collective-permute-done.21.refs_2_), channel_id=1, source_target_pairs={{0,1},{1,0},{2,3},{3,2},{4,5},{5,4},{6,7},{7,6},{8,9},{9,8},{10,11... | collective-permute-start | bytes 1179656 | tf_op jit(solution)/shard_map/ppermute | solution.py:556
  223.3 5.8 %collective-permute-start.24 = (bf16[192,1024]{1,0:T(8,128)(2,1)S(1)}, bf16[192,1024]{1,0:T(8,128)(2,1)}, u32[]{:S(2)}, u32[]{:S(2)}) collective-permute-start(bf16[192,1024]{1,0:T(8,128)(2,1)S(1)} %collective-permute-done.23.refs_4_), channel_id=1, source_target_pairs={{0,1},{1,0},{2,3},{3,2},{4,5},{5,4},{6,7},{7,6},{8,9},{9,8},{10,11... | collective-permute-start | bytes 1179656 | tf_op jit(solution)/shard_map/ppermute | solution.py:556
  229.1 1.4 collective-permute-start.26
  230.6 0.6 dynamic_slice.3
  231.2 1.7 fusion.1
  232.9 5.9 %place.1 = f32[768,2048]{1,0:T(8,128)} custom-call(s32[5]{0:T(128)S(1)} %stack.99.info_ref, bf16[192,1024]{1,0:T(8,128)(2,1)S(1)} %add.147.refs_0_, bf16[192,1024]{1,0:T(8,128)(2,1)S(1)} %collective-permute-done.20.refs_1_, bf16[192,1024]{1,0:T(8,128)(2,1)S(1)} %collective-permute-done.21.refs_2_, bf16[192,1024]{1,0:T(8,128)(2,1)} %collective-permute-done.22.refs_3_, ...), custom_call_target="tpu_custom_call" | custom-call | flops 1 | bytes 1 | tf_op jit(solution)/shard_map/place/pallas_call | solution.py:125
  (58 shorter events, 1.6 us)
Async XLA Ops:
  1.4 2.8 %copy-start = (bf16[1,256,2048]{2,1,0:T(8,128)(2,1)S(1)}, bf16[1,256,2048]{2,1,0:T(8,128)(2,1)}, u32[]{:S(2)}) copy-start(bf16[1,256,2048]{2,1,0:T(8,128)(2,1)} %param.16) | copy-start | bytes 3145732
  1.4 1.1 copy-start.5
  2.5 1.0 copy-start.6
  3.6 1.1 copy-start.10
  4.7 16.1 %copy-start.4 = (bf16[1,256,5120]{2,1,0:T(8,128)(2,1)S(1)}, bf16[1,256,5120]{2,1,0:T(8,128)(2,1)}, u32[]{:S(2)}) copy-start(bf16[1,256,5120]{2,1,0:T(8,128)(2,1)} %param.9) | copy-start | bytes 7864324
  9.2 41.5 %collective-permute-start.9 = (bf16[1536,1024]{1,0:T(8,128)(2,1)}, bf16[1536,1024]{1,0:T(8,128)(2,1)}, u32[]{:S(2)}, u32[]{:S(2)}) collective-permute-start(bf16[1536,1024]{1,0:T(8,128)(2,1)} %get-tuple-element.21.refs_0_), channel_id=1, source_target_pairs={{0,1},{1,0},{2,3},{3,2},{4,5},{5,4},{6,7},{7,6},{8,9},{9,8},{10,11... | collective-permute-start | bytes 9437192 | tf_op jit(solution)/shard_map/ppermute | solution.py:461
  10.6 5.9 %collective-permute-start.1 = (bf16[2,256,512]{2,1,0:T(8,128)(2,1)S(1)}, bf16[2,256,512]{2,1,0:T(8,128)(2,1)S(1)}, u32[]{:S(2)}, u32[]{:S(2)}) collective-permute-start(bf16[2,256,512]{2,1,0:T(8,128)(2,1)S(1)} %get-tuple-element.22), channel_id=1, source_target_pairs={{0,1},{1,0},{2,3},{3,2},{4,5},{5,4},{6,7},{7,6},{8,9},{9,8},{10,11... | collective-permute-start | bytes 1572872 | tf_op jit(solution)/shard_map/ppermute | solution.py:425
  17.4 26.0 %collective-permute-start.2 = (bf16[2,512,512]{2,1,0:T(8,128)(2,1)}, bf16[2,512,512]{2,1,0:T(8,128)(2,1)S(1)}, u32[]{:S(2)}, u32[]{:S(2)}) collective-permute-start(bf16[2,512,512]{2,1,0:T(8,128)(2,1)} %constant_dynamic-update-slice_fusion.refs_8_.refs_9_), channel_id=1, source_target_pairs={{0,8},{1,9},{2,10},{3,11},{4,12},{5,13},{6,14},{7,15},{16,24},{17,... | collective-permute-start | bytes 3145736 | tf_op jit(solution)/shard_map/ppermute | solution.py:434
  22.4 35.5 %collective-permute-start = (bf16[256,2560]{1,0:T(8,128)(2,1)}, bf16[256,2560]{1,0:T(8,128)(2,1)}, u32[]{:S(2)}, u32[]{:S(2)}) collective-permute-start(bf16[256,2560]{1,0:T(8,128)(2,1)} %pick.2), channel_id=1, source_target_pairs={{0,1},{1,0},{2,3},{3,2},{4,5},{5,4},{6,7},{7,6},{8,9},{9,8},{10,11... | collective-permute-start | bytes 3932168 | tf_op jit(solution)/shard_map/ppermute | solution.py:431
  22.9 35.8 %collective-permute-start.6 = (bf16[2,512,512]{2,1,0:T(8,128)(2,1)}, bf16[2,512,512]{2,1,0:T(8,128)(2,1)}, u32[]{:S(2)}, u32[]{:S(2)}) collective-permute-start(bf16[2,512,512]{2,1,0:T(8,128)(2,1)} %constant_dynamic-update-slice_fusion.refs_8_.refs_9_), channel_id=1, source_target_pairs={{0,2},{1,3},{2,4},{3,5},{4,6},{5,7},{6,0},{7,1},{8,10},{9,11},{10,... | collective-permute-start | bytes 3145736 | tf_op jit(solution)/shard_map/ppermute | solution.py:411
  24.1 35.3 %collective-permute-start.7 = (bf16[2,512,512]{2,1,0:T(8,128)(2,1)}, bf16[2,512,512]{2,1,0:T(8,128)(2,1)}, u32[]{:S(2)}, u32[]{:S(2)}) collective-permute-start(bf16[2,512,512]{2,1,0:T(8,128)(2,1)} %constant_dynamic-update-slice_fusion.refs_8_.refs_9_), channel_id=1, source_target_pairs={{0,6},{1,7},{2,0},{3,1},{4,2},{5,3},{6,4},{7,5},{8,14},{9,15},{10,... | collective-permute-start | bytes 3145736 | tf_op jit(solution)/shard_map/ppermute | solution.py:411
  43.4 1.0 copy-start.7
  44.5 28.1 %collective-permute-start.8 = (bf16[2,512,512]{2,1,0:T(8,128)(2,1)}, bf16[2,512,512]{2,1,0:T(8,128)(2,1)}, u32[]{:S(2)}, u32[]{:S(2)}) collective-permute-start(bf16[2,512,512]{2,1,0:T(8,128)(2,1)} %constant_dynamic-update-slice_fusion.refs_8_.refs_9_), channel_id=1, source_target_pairs={{0,4},{1,5},{2,6},{3,7},{4,0},{5,1},{6,2},{7,3},{8,12},{9,13},{10,... | collective-permute-start | bytes 3145736 | tf_op jit(solution)/shard_map/ppermute | solution.py:411
  47.4 7.1 %copy-start.8 = (bf16[2,512,512]{2,1,0:T(8,128)(2,1)S(1)}, bf16[2,512,512]{2,1,0:T(8,128)(2,1)}, u32[]{:S(2)}) copy-start(bf16[2,512,512]{2,1,0:T(8,128)(2,1)} %copy-done.7) | copy-start | bytes 3145732
  50.7 21.9 %copy-start.2 = (f32[256,768]{1,0:T(8,128)}, f32[256,768]{1,0:T(8,128)S(1)}, u32[]{:S(2)}) copy-start(f32[256,768]{1,0:T(8,128)S(1)} %fusion.3.refs_11_.refs_4_) | copy-start | bytes 2359300
  50.7 86.1 %collective-permute-start.15 = (bf16[768,2048]{1,0:T(8,128)(2,1)}, bf16[768,2048]{1,0:T(8,128)(2,1)}, u32[]{:S(2)}, u32[]{:S(2)}) collective-permute-start(bf16[768,2048]{1,0:T(8,128)(2,1)} %param.17), channel_id=1, source_target_pairs={{0,24},{8,16},{16,8},{24,0},{32,56},{40,48},{48,40},{56,32},{64,88... | collective-permute-start | bytes 9437192 | tf_op jit(solution)/shard_map/ppermute | solution.py:444
  57.9 51.8 %collective-permute-start.3 = (bf16[2,512,512]{2,1,0:T(8,128)(2,1)S(1)}, bf16[2,512,512]{2,1,0:T(8,128)(2,1)S(1)}, u32[]{:S(2)}, u32[]{:S(2)}) collective-permute-start(bf16[2,512,512]{2,1,0:T(8,128)(2,1)S(1)} %copy-done.8), channel_id=1, source_target_pairs={{8,10},{9,11},{10,12},{11,13},{12,14},{13,15},{14,8},{15,9},{24,26... | collective-permute-start | bytes 3145736 | tf_op jit(solution)/shard_map/ppermute | solution.py:411
  58.7 57.0 %collective-permute-start.4 = (bf16[2,512,512]{2,1,0:T(8,128)(2,1)S(1)}, bf16[2,512,512]{2,1,0:T(8,128)(2,1)S(1)}, u32[]{:S(2)}, u32[]{:S(2)}) collective-permute-start(bf16[2,512,512]{2,1,0:T(8,128)(2,1)S(1)} %copy-done.8), channel_id=1, source_target_pairs={{8,14},{9,15},{10,8},{11,9},{12,10},{13,11},{14,12},{15,13},{24,30... | collective-permute-start | bytes 3145736 | tf_op jit(solution)/shard_map/ppermute | solution.py:411
  59.4 56.3 %collective-permute-start.5 = (bf16[2,512,512]{2,1,0:T(8,128)(2,1)S(1)}, bf16[2,512,512]{2,1,0:T(8,128)(2,1)S(1)}, u32[]{:S(2)}, u32[]{:S(2)}) collective-permute-start(bf16[2,512,512]{2,1,0:T(8,128)(2,1)S(1)} %copy-done.8), channel_id=1, source_target_pairs={{8,12},{9,13},{10,14},{11,15},{12,8},{13,9},{14,10},{15,11},{24,28... | collective-permute-start | bytes 3145736 | tf_op jit(solution)/shard_map/ppermute | solution.py:411
  72.6 34.9 %collective-permute-start.10 = (bf16[768,1024]{1,0:T(8,128)(2,1)S(1)}, bf16[768,1024]{1,0:T(8,128)(2,1)S(1)}, u32[]{:S(2)}, u32[]{:S(2)}) collective-permute-start(bf16[768,1024]{1,0:T(8,128)(2,1)S(1)} %get-tuple-element.24.refs_10_), channel_id=1, source_target_pairs={{0,8},{8,0},{1,9},{9,1},{2,10},{10,2},{3,11},{11,3},{4,12},{12,4},... | collective-permute-start | bytes 4718600 | tf_op jit(solution)/shard_map/ppermute | solution.py:472
  107.5 1.2 copy-start.9
  109.6 16.3 %collective-permute-start.11 = (bf16[192,1024]{1,0:T(8,128)(2,1)S(1)}, bf16[192,1024]{1,0:T(8,128)(2,1)S(1)}, u32[]{:S(2)}, u32[]{:S(2)}) collective-permute-start(bf16[192,1024]{1,0:T(8,128)(2,1)S(1)} %get-tuple-element.31), channel_id=1, source_target_pairs={{0,2},{1,3},{2,4},{3,5},{4,6},{5,7},{6,0},{7,1},{8,10},{9,11},{10,... | collective-permute-start | bytes 1179656 | tf_op jit(solution)/shard_map/ppermute | solution.py:411
  109.7 6.0 %copy-start.13 = (bf16[2,512,512]{2,1,0:T(8,128)(2,1)}, bf16[2,512,512]{2,1,0:T(8,128)(2,1)S(1)}, u32[]{:S(2)}) copy-start(bf16[2,512,512]{2,1,0:T(8,128)(2,1)S(1)} %collective-permute-done.3.refs_0_.refs_1_) | copy-start | bytes 3145732
  109.7 20.2 %collective-permute-start.12 = (bf16[192,1024]{1,0:T(8,128)(2,1)S(1)}, bf16[192,1024]{1,0:T(8,128)(2,1)S(1)}, u32[]{:S(2)}, u32[]{:S(2)}) collective-permute-start(bf16[192,1024]{1,0:T(8,128)(2,1)S(1)} %get-tuple-element.32), channel_id=1, source_target_pairs={{0,4},{1,5},{2,6},{3,7},{4,0},{5,1},{6,2},{7,3},{8,12},{9,13},{10,... | collective-permute-start | bytes 1179656 | tf_op jit(solution)/shard_map/ppermute | solution.py:411
  115.7 1.0 copy-start.14
  115.7 16.4 %collective-permute-start.13 = (bf16[192,1024]{1,0:T(8,128)(2,1)S(1)}, bf16[192,1024]{1,0:T(8,128)(2,1)S(1)}, u32[]{:S(2)}, u32[]{:S(2)}) collective-permute-start(bf16[192,1024]{1,0:T(8,128)(2,1)S(1)} %get-tuple-element.33), channel_id=1, source_target_pairs={{0,6},{1,7},{2,0},{3,1},{4,2},{5,3},{6,4},{7,5},{8,14},{9,15},{10,... | collective-permute-start | bytes 1179656 | tf_op jit(solution)/shard_map/ppermute | solution.py:411
  115.7 1.3 copy-start.15
  132.8 6.8 %copy-start.11 = (f32[5120]{0:T(1024)S(1)}, f32[5120]{0:T(1024)}, u32[]{:S(2)}) copy-start(f32[5120]{0:T(1024)} %param.13) | copy-start | bytes 61444
  132.9 6.8 %copy-start.12 = (f32[5120]{0:T(1024)S(1)}, f32[5120]{0:T(1024)}, u32[]{:S(2)}) copy-start(f32[5120]{0:T(1024)} %param.14) | copy-start | bytes 61444
  134.6 5.1 %collective-permute-start.14 = (bf16[256,2560]{1,0:T(8,128)(2,1)}, bf16[256,2560]{1,0:T(8,128)(2,1)}, u32[]{:S(2)}, u32[]{:S(2)}) collective-permute-start(bf16[256,2560]{1,0:T(8,128)(2,1)} %pick.3), channel_id=1, source_target_pairs={{0,1},{1,0},{2,3},{3,2},{4,5},{5,4},{6,7},{7,6},{8,9},{9,8},{10,11... | collective-permute-start | bytes 3932168 | tf_op jit(solution)/shard_map/ppermute | solution.py:525
  139.6 31.1 %copy-start.1 = (bf16[1,256,2048]{2,1,0:T(8,128)(2,1)S(1)}, bf16[1,256,2048]{2,1,0:T(8,128)(2,1)}, u32[]{:S(2)}) copy-start(bf16[1,256,2048]{2,1,0:T(8,128)(2,1)} %param.16) | copy-start | bytes 3145732
  144.5 35.5 %all-to-all-start = ((f32[128,1,128]{2,1,0:T(1,128)}), f32[128,1,128]{2,1,0:T(1,128)}, u32[]{:S(2)}, u32[]{:S(2)}) async-start(f32[128,1,128]{2,1,0:T(1,128)} %broadcast_in_dim.34), calls=%async_computation | async-start | bytes 131072 | tf_op jit(solution)/shard_map/all_to_all | solution.py:535
  170.7 25.2 %copy-start.3 = (f32[256,768]{1,0:T(8,128)S(1)}, f32[256,768]{1,0:T(8,128)}, u32[]{:S(2)}) copy-start(f32[256,768]{1,0:T(8,128)} %copy-done.2) | copy-start | bytes 2359300
  173.7 12.6 %collective-permute-start.16 = (bf16[192,1024]{1,0:T(8,128)(2,1)S(1)}, bf16[192,1024]{1,0:T(8,128)(2,1)S(1)}, u32[]{:S(2)}, u32[]{:S(2)}) collective-permute-start(bf16[192,1024]{1,0:T(8,128)(2,1)S(1)} %add.146.refs_0_), channel_id=1, source_target_pairs={{0,32},{16,48},{32,64},{48,80},{64,96},{80,112},{96,0},{112,16},{1... | collective-permute-start | bytes 1179656 | tf_op jit(solution)/shard_map/ppermute | solution.py:518
  175.6 20.4 %collective-permute-start.17 = (bf16[192,1024]{1,0:T(8,128)(2,1)S(1)}, bf16[192,1024]{1,0:T(8,128)(2,1)S(1)}, u32[]{:S(2)}, u32[]{:S(2)}) collective-permute-start(bf16[192,1024]{1,0:T(8,128)(2,1)S(1)} %add.146.refs_0_), channel_id=1, source_target_pairs={{0,64},{16,80},{32,96},{48,112},{64,0},{80,16},{96,32},{112,48},{1... | collective-permute-start | bytes 1179656 | tf_op jit(solution)/shard_map/ppermute | solution.py:518
  178.5 17.5 %collective-permute-start.18 = (bf16[192,1024]{1,0:T(8,128)(2,1)S(1)}, bf16[192,1024]{1,0:T(8,128)(2,1)S(1)}, u32[]{:S(2)}, u32[]{:S(2)}) collective-permute-start(bf16[192,1024]{1,0:T(8,128)(2,1)S(1)} %add.146.refs_0_), channel_id=1, source_target_pairs={{0,96},{16,112},{32,0},{48,16},{64,32},{80,48},{96,64},{112,80},{1... | collective-permute-start | bytes 1179656 | tf_op jit(solution)/shard_map/ppermute | solution.py:518
  196.9 11.1 %collective-permute-start.19 = (bf16[192,1024]{1,0:T(8,128)(2,1)S(1)}, bf16[192,1024]{1,0:T(8,128)(2,1)S(1)}, u32[]{:S(2)}, u32[]{:S(2)}) collective-permute-start(bf16[192,1024]{1,0:T(8,128)(2,1)S(1)} %combine.1.refs_0_), channel_id=1, source_target_pairs={{0,16},{16,0},{32,48},{48,32},{64,80},{80,64},{96,112},{112,96},{1... | collective-permute-start | bytes 1179656 | tf_op jit(solution)/shard_map/ppermute | solution.py:549
  208.6 9.8 %collective-permute-start.21 = (bf16[192,1024]{1,0:T(8,128)(2,1)S(1)}, bf16[192,1024]{1,0:T(8,128)(2,1)S(1)}, u32[]{:S(2)}, u32[]{:S(2)}) collective-permute-start(bf16[192,1024]{1,0:T(8,128)(2,1)S(1)} %add.147.refs_0_), channel_id=1, source_target_pairs={{0,2},{1,3},{2,4},{3,5},{4,6},{5,7},{6,0},{7,1},{8,10},{9,11},{10,... | collective-permute-start | bytes 1179656 | tf_op jit(solution)/shard_map/ppermute | solution.py:411
  209.7 13.6 %collective-permute-start.23 = (bf16[192,1024]{1,0:T(8,128)(2,1)S(1)}, bf16[192,1024]{1,0:T(8,128)(2,1)S(1)}, u32[]{:S(2)}, u32[]{:S(2)}) collective-permute-start(bf16[192,1024]{1,0:T(8,128)(2,1)S(1)} %add.147.refs_0_), channel_id=1, source_target_pairs={{0,6},{1,7},{2,0},{3,1},{4,2},{5,3},{6,4},{7,5},{8,14},{9,15},{10,... | collective-permute-start | bytes 1179656 | tf_op jit(solution)/shard_map/ppermute | solution.py:411
  211.3 17.8 %collective-permute-start.25 = (bf16[192,1024]{1,0:T(8,128)(2,1)S(1)}, bf16[192,1024]{1,0:T(8,128)(2,1)S(1)}, u32[]{:S(2)}, u32[]{:S(2)}) collective-permute-start(bf16[192,1024]{1,0:T(8,128)(2,1)S(1)} %add.147.refs_0_), channel_id=1, source_target_pairs={{0,4},{1,5},{2,6},{3,7},{4,0},{5,1},{6,2},{7,3},{8,12},{9,13},{10,... | collective-permute-start | bytes 1179656 | tf_op jit(solution)/shard_map/ppermute | solution.py:411
  212.6 20.3 %collective-permute-start.20 = (bf16[192,1024]{1,0:T(8,128)(2,1)S(1)}, bf16[192,1024]{1,0:T(8,128)(2,1)S(1)}, u32[]{:S(2)}, u32[]{:S(2)}) collective-permute-start(bf16[192,1024]{1,0:T(8,128)(2,1)S(1)} %add.147.refs_0_), channel_id=1, source_target_pairs={{0,1},{1,0},{2,3},{3,2},{4,5},{5,4},{6,7},{7,6},{8,9},{9,8},{10,11... | collective-permute-start | bytes 1179656 | tf_op jit(solution)/shard_map/ppermute | solution.py:556
  218.4 14.5 %collective-permute-start.22 = (bf16[192,1024]{1,0:T(8,128)(2,1)S(1)}, bf16[192,1024]{1,0:T(8,128)(2,1)}, u32[]{:S(2)}, u32[]{:S(2)}) collective-permute-start(bf16[192,1024]{1,0:T(8,128)(2,1)S(1)} %collective-permute-done.21.refs_2_), channel_id=1, source_target_pairs={{0,1},{1,0},{2,3},{3,2},{4,5},{5,4},{6,7},{7,6},{8,9},{9,8},{10,11... | collective-permute-start | bytes 1179656 | tf_op jit(solution)/shard_map/ppermute | solution.py:556
  223.3 9.6 %collective-permute-start.24 = (bf16[192,1024]{1,0:T(8,128)(2,1)S(1)}, bf16[192,1024]{1,0:T(8,128)(2,1)}, u32[]{:S(2)}, u32[]{:S(2)}) collective-permute-start(bf16[192,1024]{1,0:T(8,128)(2,1)S(1)} %collective-permute-done.23.refs_4_), channel_id=1, source_target_pairs={{0,1},{1,0},{2,3},{3,2},{4,5},{5,4},{6,7},{7,6},{8,9},{9,8},{10,11... | collective-permute-start | bytes 1179656 | tf_op jit(solution)/shard_map/ppermute | solution.py:556
  229.1 3.8 %collective-permute-start.26 = (bf16[192,1024]{1,0:T(8,128)(2,1)S(1)}, bf16[192,1024]{1,0:T(8,128)(2,1)}, u32[]{:S(2)}, u32[]{:S(2)}) collective-permute-start(bf16[192,1024]{1,0:T(8,128)(2,1)S(1)} %collective-permute-done.25.refs_6_), channel_id=1, source_target_pairs={{0,1},{1,0},{2,3},{3,2},{4,5},{5,4},{6,7},{7,6},{8,9},{9,8},{10,11... | collective-permute-start | bytes 1179656 | tf_op jit(solution)/shard_map/ppermute | solution.py:556
